TPU v7x, 1024 devices: a whole 4x4x32 slice. The times are simulated.
1024 devices in a mesh: we: 8 (over x_lo, y), sn: 128 (over x_hi, z, core).
Axes of the slice: x: 4 (x_hi: 2, x_lo: 2; x = x_hi * 2 + x_lo), y: 4, z: 32, core: 2. Of those that a mesh axis runs over, the one named last changes fastest.
Arguments:
- velocity: float32 [3, 32, 1536, 128], P(None, 'we', 'sn'), may hold values from -6 to 6
- stress: float32 [6, 32, 1536, 128], P(None, 'we', 'sn'), may hold values from -6 to 6
- memory: float32 [6, 32, 1536, 128], P(None, 'we', 'sn'), may hold values from -3 to 3
- material_code: int32 [32, 1536, 128], P('we', 'sn'), may hold values from 0 to 15
- block_scale: float32 [8, 384, 4], P('we', 'sn'), may hold values from 0.5 to 2
- material_table: float32 [6, 16], replicated, may hold values from 0.2 to 3, as said below
- source_cell: int32 [8, 128, 4], P('we', 'sn'), may hold values from 0 to 6143, as said below
- source_amp: float32 [8, 128, 4, 4], P('we', 'sn'), may hold values from -24 to 24
Outputs:
- velocity_out: float32 [3, 32, 1536, 128], P(None, 'we', 'sn')
- stress_out: float32 [6, 32, 1536, 128], P(None, 'we', 'sn')
- memory_out: float32 [6, 32, 1536, 128], P(None, 'we', 'sn')
Inputs may be any that keep to these rules, and one draw needn't show every extreme that they name: Rows of material_table lie in: buoyancy 0.6 to 1.4, first Lame parameter 0.5 to 2, shear modulus 0.3 to 1.5, decay 0.5 to 0.98, weight 0.2 to 0.8, cohesion 0.3 to 3. `source_cell`: each entry is c = x 12 * 128 + y * 128 + z for a cell (x, y, z) of the device's own block; cells may repeat.
All inputs are finite; a program needn't handle non-finite values.
Results may differ from a plain program's by a relative error of at most 0.0001.
Values sent between devices are 32-bit elements; how exact they have to be, the bound alone decides.
A program may use at most 32 MiB of HBM per device.

v0:
```python
import jax
import jax.numpy as jnp
from jax import lax
from jax.sharding import PartitionSpec as P

STEPS = 4
BLK = 4
BLKZ = 32


inner_coef = 9.0 / 8.0
outer_coef = 1.0 / 24.0
time_step = 0.08
friction = 0.4


def with_halo(block, sides, width):
    for axis, dim in sides:
        count = lax.axis_size(axis)
        forward = [(i, i + 1) for i in range(count - 1)]
        backward = [(target, source) for source, target in forward]
        low = lax.ppermute(
            lax.slice_in_dim(block, block.shape[dim] - width, None, axis=dim), axis, forward
        )
        high = lax.ppermute(lax.slice_in_dim(block, 0, width, axis=dim), axis, backward)
        block = jnp.concatenate([low, block, high], axis=dim)
    return block


def shifted(padded, along_dim, offset):
    length = padded.shape[along_dim] - 4
    return lax.slice_in_dim(padded, 2 + offset, 2 + offset + length, axis=along_dim)


def forward(padded, along_dim):
    return inner_coef * (
        shifted(padded, along_dim, 1) - shifted(padded, along_dim, 0)
    ) - outer_coef * (shifted(padded, along_dim, 2) - shifted(padded, along_dim, -1))


def backward(padded, along_dim):
    return inner_coef * (
        shifted(padded, along_dim, 0) - shifted(padded, along_dim, -1)
    ) - outer_coef * (shifted(padded, along_dim, 1) - shifted(padded, along_dim, -2))


def depth_pad(fields):
    return jnp.pad(fields, ((0, 0), (0, 0), (0, 0), (2, 2)))


def velocity_step(velocity, stress, east_pad, north_pad, buoyancy):
    depth_stress = depth_pad(stress[1::2])
    force_east = forward(east_pad[0], 0) + backward(north_pad[0], 1) + backward(depth_stress[0], 2)
    force_north = backward(east_pad[2], 0) + forward(north_pad[2], 1) + backward(depth_stress[1], 2)
    force_depth = backward(east_pad[1], 0) + backward(north_pad[1], 1) + forward(depth_stress[2], 2)
    return velocity + time_step * buoyancy * jnp.stack([force_east, force_north, force_depth])


def stress_step(stress, memory, east_vel, north_vel, velocity, lame, shear_mod, decay, weight):
    depth_vel = depth_pad(velocity)
    rate_ee = backward(east_vel[0], 0)
    north_east = forward(east_vel[1], 0)
    depth_east = forward(east_vel[2], 0)
    east_north = forward(north_vel[0], 1)
    rate_nn = backward(north_vel[1], 1)
    depth_north = forward(north_vel[2], 1)
    east_depth = forward(depth_vel[0], 2)
    north_depth = forward(depth_vel[1], 2)
    rate_dd = backward(depth_vel[2], 2)
    volume_rate = rate_ee + rate_nn + rate_dd
    rates = jnp.stack(
        [
            lame * volume_rate + 2.0 * shear_mod * rate_ee,
            shear_mod * (east_depth + depth_east),
            shear_mod * (east_north + north_east),
            shear_mod * (north_depth + depth_north),
            lame * volume_rate + 2.0 * shear_mod * rate_nn,
            lame * volume_rate + 2.0 * shear_mod * rate_dd,
        ]
    )
    memory_new = decay * memory + (1.0 - decay) * weight * rates
    trial = stress + time_step * (rates - 0.5 * (memory + memory_new))
    return (trial, memory_new)


def plastic(trial, cohesion):
    normal_mask = jnp.array([1.0, 0.0, 0.0, 0.0, 1.0, 1.0], jnp.float32)[:, None, None, None]
    square_weights = jnp.array([0.5, 1.0, 1.0, 1.0, 0.5, 0.5], jnp.float32)[:, None, None, None]
    mean_stress = (trial[0] + trial[4] + trial[5]) / 3.0
    deviator = trial - normal_mask * mean_stress
    second_inv = jnp.sum(square_weights * deviator * deviator, 0)
    yield_level = cohesion + friction * jax.nn.softplus(-mean_stress)
    scaled = second_inv / (yield_level * yield_level)
    factor = lax.rsqrt(jnp.sqrt(1.0 + scaled * scaled))
    return normal_mask * mean_stress + factor * deviator


def shards(
    velocity, stress, memory, material_code, block_scale, material_table, source_cell, source_amp
):
    entries = material_table.shape[1]
    levels = lax.broadcasted_iota(jnp.int32, (entries, 1, 1, 1), 0)
    one_hot = (material_code[None] == levels).astype(jnp.float32)
    table_rows = jnp.tensordot(material_table, one_hot, axes=1, precision=lax.Precision.HIGHEST)
    scale_full = jnp.repeat(jnp.repeat(jnp.repeat(block_scale, BLK, 0), BLK, 1), BLKZ, 2)
    buoyancy = table_rows[0]
    lame = table_rows[1] * scale_full
    shear_mod = table_rows[2] * scale_full
    decay = table_rows[3]
    weight = table_rows[4]
    cohesion = table_rows[5]
    source_cells = source_cell.reshape(-1)
    strengths = source_amp.reshape(-1, source_amp.shape[-1])
    normal_rows = jnp.array([0, 4, 5], jnp.int32)
    for turn_index in range(STEPS):
        padded = with_halo(stress, (("we", 1), ("sn", 2)), 2)
        east_pad = padded[0:3, :, 2:-2]
        north_pad = padded[2:5, 2:-2]
        velocity = velocity_step(velocity, stress, east_pad, north_pad, buoyancy)
        moved = with_halo(velocity, (("we", 1), ("sn", 2)), 2)
        east_vel = moved[:, :, 2:-2]
        north_vel = moved[:, 2:-2]
        trial, memory = stress_step(
            stress, memory, east_vel, north_vel, velocity, lame, shear_mod, decay, weight
        )
        flat = trial.reshape(6, -1)
        flat = flat.at[normal_rows[:, None], source_cells[None, :]].add(
            time_step * strengths[:, turn_index][None, :]
        )
        trial = flat.reshape(stress.shape)
        stress = plastic(trial, cohesion)
    return (velocity, stress, memory)


def solution(mesh):
    in_specs = (
        P(None, "we", "sn", None),
        P(None, "we", "sn", None),
        P(None, "we", "sn", None),
        P("we", "sn", None),
        P("we", "sn", None),
        P(),
        P("we", "sn", None),
        P("we", "sn", None, None),
    )
    out_specs = (P(None, "we", "sn", None), P(None, "we", "sn", None), P(None, "we", "sn", None))
    return jax.shard_map(shards, mesh=mesh, in_specs=in_specs, out_specs=out_specs, check_vma=False)
```

profile of v0, /device:TPU:6, one launch (start us, length us, event | category | flops | bytes accessed | tf_op | source)
XLA Modules:
  0.0 214.0 jit_solution(11076558602136615319)
XLA Ops:
  1.7 5.2 %collective-permute-start = (f32[6,2,12,128]{3,1,2,0:T(2,128)S(1)}, f32[6,2,12,128]{3,1,2,0:T(2,128)S(1)}, u32[]{:S(2)}, u32[]{:S(2)}) collective-permute-start(f32[6,2,12,128]{3,1,2,0:T(2,128)S(1)} %get-tuple-element.100), channel_id=1, source_target_pairs={{128,0},{256,128},{384,256},{512,384},{640,512},{768,640},{896,768... | collective-permute-start | bytes 221192 | tf_op jit(solution)/shard_map/ppermute | solution.py:25
  10.1 5.2 %collective-permute-done.1 = f32[6,2,12,128]{3,1,2,0:T(2,128)S(1)} collective-permute-done((f32[6,2,12,128]{3,1,2,0:T(2,128)S(1)}, f32[6,2,12,128]{3,1,2,0:T(2,128)S(1)}, u32[]{:S(2)}, u32[]{:S(2)}) %collective-permute-start.1) | collective-permute-done | bytes 73760 | tf_op jit(solution)/shard_map/ppermute | solution.py:22
  15.3 1.9 collective-permute-start.2
  17.2 17.2 %collective-permute-start.3 = (f32[6,8,2,128]{3,1,2,0:T(8,128)S(1)}, f32[6,8,2,128]{3,1,2,0:T(8,128)S(1)}, u32[]{:S(2)}, u32[]{:S(2)}) collective-permute-start(f32[6,8,2,128]{3,1,2,0:T(8,128)S(1)} %get-tuple-element.65), channel_id=1, source_target_pairs={{1,0},{2,1},{3,2},{4,3},{5,4},{6,5},{7,6},{8,7},{9,8},{10,9},{11,1... | collective-permute-start | bytes 147464 | tf_op jit(solution)/shard_map/ppermute | solution.py:25
  37.5 1.9 collective-permute-start.4
  39.4 6.0 %collective-permute-start.5 = (f32[3,2,12,128]{3,1,2,0:T(2,128)S(1)}, f32[3,2,12,128]{3,1,2,0:T(2,128)S(1)}, u32[]{:S(2)}, u32[]{:S(2)}) collective-permute-start(f32[3,2,12,128]{3,1,2,0:T(2,128)S(1)} %get-tuple-element.128), channel_id=1, source_target_pairs={{128,0},{256,128},{384,256},{512,384},{640,512},{768,640},{896,768... | collective-permute-start | bytes 110600 | tf_op jit(solution)/shard_map/ppermute | solution.py:25
  47.1 1.9 collective-permute-start.6
  49.0 7.3 %collective-permute-start.7 = (f32[3,8,2,128]{3,1,2,0:T(8,128)S(1)}, f32[3,8,2,128]{3,1,2,0:T(8,128)S(1)}, u32[]{:S(2)}, u32[]{:S(2)}) collective-permute-start(f32[3,8,2,128]{3,1,2,0:T(8,128)S(1)} %get-tuple-element.98), channel_id=1, source_target_pairs={{1,0},{2,1},{3,2},{4,3},{5,4},{6,5},{7,6},{8,7},{9,8},{10,9},{11,1... | collective-permute-start | bytes 73736 | tf_op jit(solution)/shard_map/ppermute | solution.py:25
  63.1 6.3 %collective-permute-start.8 = (f32[6,2,12,128]{3,1,2,0:T(2,128)S(1)}, f32[6,2,12,128]{3,1,2,0:T(2,128)S(1)}, u32[]{:S(2)}, u32[]{:S(2)}) collective-permute-start(f32[6,2,12,128]{3,1,2,0:T(2,128)S(1)} %get-tuple-element.89), channel_id=1, source_target_pairs={{128,0},{256,128},{384,256},{512,384},{640,512},{768,640},{896,768... | collective-permute-start | bytes 221192 | tf_op jit(solution)/shard_map/ppermute | solution.py:25
  69.5 1.9 collective-permute-start.9
  71.4 6.4 %collective-permute-done.9 = f32[6,2,12,128]{3,1,2,0:T(2,128)S(1)} collective-permute-done((f32[6,2,12,128]{3,1,2,0:T(2,128)S(1)}, f32[6,2,12,128]{3,1,2,0:T(2,128)S(1)}, u32[]{:S(2)}, u32[]{:S(2)}) %collective-permute-start.9) | collective-permute-done | bytes 73760 | tf_op jit(solution)/shard_map/ppermute | solution.py:22
  79.8 7.3 %collective-permute-start.11 = (f32[6,8,2,128]{3,1,2,0:T(8,128)S(1)}, f32[6,8,2,128]{3,1,2,0:T(8,128)S(1)}, u32[]{:S(2)}, u32[]{:S(2)}) collective-permute-start(f32[6,8,2,128]{3,1,2,0:T(8,128)S(1)} %get-tuple-element.63), channel_id=1, source_target_pairs={{1,0},{2,1},{3,2},{4,3},{5,4},{6,5},{7,6},{8,7},{9,8},{10,9},{11,1... | collective-permute-start | bytes 147464 | tf_op jit(solution)/shard_map/ppermute | solution.py:25
  91.2 6.0 %collective-permute-start.13 = (f32[3,2,12,128]{3,1,2,0:T(2,128)S(1)}, f32[3,2,12,128]{3,1,2,0:T(2,128)S(1)}, u32[]{:S(2)}, u32[]{:S(2)}) collective-permute-start(f32[3,2,12,128]{3,1,2,0:T(2,128)S(1)} %get-tuple-element.120), channel_id=1, source_target_pairs={{128,0},{256,128},{384,256},{512,384},{640,512},{768,640},{896,768... | collective-permute-start | bytes 110600 | tf_op jit(solution)/shard_map/ppermute | solution.py:25
  100.8 7.3 %collective-permute-start.15 = (f32[3,8,2,128]{3,1,2,0:T(8,128)S(1)}, f32[3,8,2,128]{3,1,2,0:T(8,128)S(1)}, u32[]{:S(2)}, u32[]{:S(2)}) collective-permute-start(f32[3,8,2,128]{3,1,2,0:T(8,128)S(1)} %get-tuple-element.87), channel_id=1, source_target_pairs={{1,0},{2,1},{3,2},{4,3},{5,4},{6,5},{7,6},{8,7},{9,8},{10,9},{11,1... | collective-permute-start | bytes 73736 | tf_op jit(solution)/shard_map/ppermute | solution.py:25
  113.0 6.3 %collective-permute-start.16 = (f32[6,2,12,128]{3,1,2,0:T(2,128)S(1)}, f32[6,2,12,128]{3,1,2,0:T(2,128)S(1)}, u32[]{:S(2)}, u32[]{:S(2)}) collective-permute-start(f32[6,2,12,128]{3,1,2,0:T(2,128)S(1)} %get-tuple-element.85), channel_id=1, source_target_pairs={{128,0},{256,128},{384,256},{512,384},{640,512},{768,640},{896,768... | collective-permute-start | bytes 221192 | tf_op jit(solution)/shard_map/ppermute | solution.py:25
  121.3 6.4 %collective-permute-done.17 = f32[6,2,12,128]{3,1,2,0:T(2,128)S(1)} collective-permute-done((f32[6,2,12,128]{3,1,2,0:T(2,128)S(1)}, f32[6,2,12,128]{3,1,2,0:T(2,128)S(1)}, u32[]{:S(2)}, u32[]{:S(2)}) %collective-permute-start.17) | collective-permute-done | bytes 73760 | tf_op jit(solution)/shard_map/ppermute | solution.py:22
  129.7 7.3 %collective-permute-start.19 = (f32[6,8,2,128]{3,1,2,0:T(8,128)S(1)}, f32[6,8,2,128]{3,1,2,0:T(8,128)S(1)}, u32[]{:S(2)}, u32[]{:S(2)}) collective-permute-start(f32[6,8,2,128]{3,1,2,0:T(8,128)S(1)} %get-tuple-element.61), channel_id=1, source_target_pairs={{1,0},{2,1},{3,2},{4,3},{5,4},{6,5},{7,6},{8,7},{9,8},{10,9},{11,1... | collective-permute-start | bytes 147464 | tf_op jit(solution)/shard_map/ppermute | solution.py:25
  141.1 6.0 %collective-permute-start.21 = (f32[3,2,12,128]{3,1,2,0:T(2,128)S(1)}, f32[3,2,12,128]{3,1,2,0:T(2,128)S(1)}, u32[]{:S(2)}, u32[]{:S(2)}) collective-permute-start(f32[3,2,12,128]{3,1,2,0:T(2,128)S(1)} %get-tuple-element.112), channel_id=1, source_target_pairs={{128,0},{256,128},{384,256},{512,384},{640,512},{768,640},{896,768... | collective-permute-start | bytes 110600 | tf_op jit(solution)/shard_map/ppermute | solution.py:25
  150.7 7.3 %collective-permute-start.23 = (f32[3,8,2,128]{3,1,2,0:T(8,128)S(1)}, f32[3,8,2,128]{3,1,2,0:T(8,128)S(1)}, u32[]{:S(2)}, u32[]{:S(2)}) collective-permute-start(f32[3,8,2,128]{3,1,2,0:T(8,128)S(1)} %get-tuple-element.83), channel_id=1, source_target_pairs={{1,0},{2,1},{3,2},{4,3},{5,4},{6,5},{7,6},{8,7},{9,8},{10,9},{11,1... | collective-permute-start | bytes 73736 | tf_op jit(solution)/shard_map/ppermute | solution.py:25
  162.8 6.3 %collective-permute-start.24 = (f32[6,2,12,128]{3,1,2,0:T(2,128)S(1)}, f32[6,2,12,128]{3,1,2,0:T(2,128)S(1)}, u32[]{:S(2)}, u32[]{:S(2)}) collective-permute-start(f32[6,2,12,128]{3,1,2,0:T(2,128)S(1)} %get-tuple-element.81), channel_id=1, source_target_pairs={{128,0},{256,128},{384,256},{512,384},{640,512},{768,640},{896,768... | collective-permute-start | bytes 221192 | tf_op jit(solution)/shard_map/ppermute | solution.py:25
  171.1 6.4 %collective-permute-done.25 = f32[6,2,12,128]{3,1,2,0:T(2,128)S(1)} collective-permute-done((f32[6,2,12,128]{3,1,2,0:T(2,128)S(1)}, f32[6,2,12,128]{3,1,2,0:T(2,128)S(1)}, u32[]{:S(2)}, u32[]{:S(2)}) %collective-permute-start.25) | collective-permute-done | bytes 73760 | tf_op jit(solution)/shard_map/ppermute | solution.py:22
  179.5 7.3 %collective-permute-start.27 = (f32[6,8,2,128]{3,1,2,0:T(8,128)S(1)}, f32[6,8,2,128]{3,1,2,0:T(8,128)S(1)}, u32[]{:S(2)}, u32[]{:S(2)}) collective-permute-start(f32[6,8,2,128]{3,1,2,0:T(8,128)S(1)} %get-tuple-element.59), channel_id=1, source_target_pairs={{1,0},{2,1},{3,2},{4,3},{5,4},{6,5},{7,6},{8,7},{9,8},{10,9},{11,1... | collective-permute-start | bytes 147464 | tf_op jit(solution)/shard_map/ppermute | solution.py:25
  191.0 6.0 %collective-permute-start.29 = (f32[3,2,12,128]{3,1,2,0:T(2,128)S(1)}, f32[3,2,12,128]{3,1,2,0:T(2,128)S(1)}, u32[]{:S(2)}, u32[]{:S(2)}) collective-permute-start(f32[3,2,12,128]{3,1,2,0:T(2,128)S(1)} %get-tuple-element.104), channel_id=1, source_target_pairs={{128,0},{256,128},{384,256},{512,384},{640,512},{768,640},{896,768... | collective-permute-start | bytes 110600 | tf_op jit(solution)/shard_map/ppermute | solution.py:25
  200.6 7.3 %collective-permute-start.31 = (f32[3,8,2,128]{3,1,2,0:T(8,128)S(1)}, f32[3,8,2,128]{3,1,2,0:T(8,128)S(1)}, u32[]{:S(2)}, u32[]{:S(2)}) collective-permute-start(f32[3,8,2,128]{3,1,2,0:T(8,128)S(1)} %get-tuple-element.79), channel_id=1, source_target_pairs={{1,0},{2,1},{3,2},{4,3},{5,4},{6,5},{7,6},{8,7},{9,8},{10,9},{11,1... | collective-permute-start | bytes 73736 | tf_op jit(solution)/shard_map/ppermute | solution.py:25
  (216 shorter events, 63.8 us)
Async XLA Ops:
  1.7 8.4 %collective-permute-start = (f32[6,2,12,128]{3,1,2,0:T(2,128)S(1)}, f32[6,2,12,128]{3,1,2,0:T(2,128)S(1)}, u32[]{:S(2)}, u32[]{:S(2)}) collective-permute-start(f32[6,2,12,128]{3,1,2,0:T(2,128)S(1)} %get-tuple-element.100), channel_id=1, source_target_pairs={{128,0},{256,128},{384,256},{512,384},{640,512},{768,640},{896,768... | collective-permute-start | bytes 221192 | tf_op jit(solution)/shard_map/ppermute | solution.py:25
  6.9 8.4 %collective-permute-start.1 = (f32[6,2,12,128]{3,1,2,0:T(2,128)S(1)}, f32[6,2,12,128]{3,1,2,0:T(2,128)S(1)}, u32[]{:S(2)}, u32[]{:S(2)}) collective-permute-start(f32[6,2,12,128]{3,1,2,0:T(2,128)S(1)} %get-tuple-element.99), channel_id=1, source_target_pairs={{0,128},{128,256},{256,384},{384,512},{512,640},{640,768},{768,896... | collective-permute-start | bytes 221192 | tf_op jit(solution)/shard_map/ppermute | solution.py:22
  15.3 19.3 %collective-permute-start.2 = (f32[6,8,2,128]{3,1,2,0:T(8,128)S(1)}, f32[6,8,2,128]{3,1,2,0:T(8,128)S(1)}, u32[]{:S(2)}, u32[]{:S(2)}) collective-permute-start(f32[6,8,2,128]{3,1,2,0:T(8,128)S(1)} %get-tuple-element.64), channel_id=1, source_target_pairs={{0,1},{1,2},{2,3},{3,4},{4,5},{5,6},{6,7},{7,8},{8,9},{9,10},{10,1... | collective-permute-start | bytes 147464 | tf_op jit(solution)/shard_map/ppermute | solution.py:22
  17.2 19.0 %collective-permute-start.3 = (f32[6,8,2,128]{3,1,2,0:T(8,128)S(1)}, f32[6,8,2,128]{3,1,2,0:T(8,128)S(1)}, u32[]{:S(2)}, u32[]{:S(2)}) collective-permute-start(f32[6,8,2,128]{3,1,2,0:T(8,128)S(1)} %get-tuple-element.65), channel_id=1, source_target_pairs={{1,0},{2,1},{3,2},{4,3},{5,4},{6,5},{7,6},{8,7},{9,8},{10,9},{11,1... | collective-permute-start | bytes 147464 | tf_op jit(solution)/shard_map/ppermute | solution.py:25
  37.5 9.3 %collective-permute-start.4 = (f32[3,2,12,128]{3,1,2,0:T(2,128)S(1)}, f32[3,2,12,128]{3,1,2,0:T(2,128)S(1)}, u32[]{:S(2)}, u32[]{:S(2)}) collective-permute-start(f32[3,2,12,128]{3,1,2,0:T(2,128)S(1)} %get-tuple-element.129), channel_id=1, source_target_pairs={{0,128},{128,256},{256,384},{384,512},{512,640},{640,768},{768,896... | collective-permute-start | bytes 110600 | tf_op jit(solution)/shard_map/ppermute | solution.py:22
  47.1 9.3 %collective-permute-start.6 = (f32[3,8,2,128]{3,1,2,0:T(8,128)S(1)}, f32[3,8,2,128]{3,1,2,0:T(8,128)S(1)}, u32[]{:S(2)}, u32[]{:S(2)}) collective-permute-start(f32[3,8,2,128]{3,1,2,0:T(8,128)S(1)} %get-tuple-element.97), channel_id=1, source_target_pairs={{0,1},{1,2},{2,3},{3,4},{4,5},{5,6},{6,7},{7,8},{8,9},{9,10},{10,1... | collective-permute-start | bytes 73736 | tf_op jit(solution)/shard_map/ppermute | solution.py:22
  49.0 8.8 %collective-permute-start.7 = (f32[3,8,2,128]{3,1,2,0:T(8,128)S(1)}, f32[3,8,2,128]{3,1,2,0:T(8,128)S(1)}, u32[]{:S(2)}, u32[]{:S(2)}) collective-permute-start(f32[3,8,2,128]{3,1,2,0:T(8,128)S(1)} %get-tuple-element.98), channel_id=1, source_target_pairs={{1,0},{2,1},{3,2},{4,3},{5,4},{6,5},{7,6},{8,7},{9,8},{10,9},{11,1... | collective-permute-start | bytes 73736 | tf_op jit(solution)/shard_map/ppermute | solution.py:25
  63.1 8.3 %collective-permute-start.8 = (f32[6,2,12,128]{3,1,2,0:T(2,128)S(1)}, f32[6,2,12,128]{3,1,2,0:T(2,128)S(1)}, u32[]{:S(2)}, u32[]{:S(2)}) collective-permute-start(f32[6,2,12,128]{3,1,2,0:T(2,128)S(1)} %get-tuple-element.89), channel_id=1, source_target_pairs={{128,0},{256,128},{384,256},{512,384},{640,512},{768,640},{896,768... | collective-permute-start | bytes 221192 | tf_op jit(solution)/shard_map/ppermute | solution.py:25
  69.5 8.4 %collective-permute-start.9 = (f32[6,2,12,128]{3,1,2,0:T(2,128)S(1)}, f32[6,2,12,128]{3,1,2,0:T(2,128)S(1)}, u32[]{:S(2)}, u32[]{:S(2)}) collective-permute-start(f32[6,2,12,128]{3,1,2,0:T(2,128)S(1)} %get-tuple-element.88), channel_id=1, source_target_pairs={{0,128},{128,256},{256,384},{384,512},{512,640},{640,768},{768,896... | collective-permute-start | bytes 221192 | tf_op jit(solution)/shard_map/ppermute | solution.py:22
  77.9 9.3 %collective-permute-start.10 = (f32[6,8,2,128]{3,1,2,0:T(8,128)S(1)}, f32[6,8,2,128]{3,1,2,0:T(8,128)S(1)}, u32[]{:S(2)}, u32[]{:S(2)}) collective-permute-start(f32[6,8,2,128]{3,1,2,0:T(8,128)S(1)} %get-tuple-element.62), channel_id=1, source_target_pairs={{0,1},{1,2},{2,3},{3,4},{4,5},{5,6},{6,7},{7,8},{8,9},{9,10},{10,1... | collective-permute-start | bytes 147464 | tf_op jit(solution)/shard_map/ppermute | solution.py:22
  79.8 9.0 %collective-permute-start.11 = (f32[6,8,2,128]{3,1,2,0:T(8,128)S(1)}, f32[6,8,2,128]{3,1,2,0:T(8,128)S(1)}, u32[]{:S(2)}, u32[]{:S(2)}) collective-permute-start(f32[6,8,2,128]{3,1,2,0:T(8,128)S(1)} %get-tuple-element.63), channel_id=1, source_target_pairs={{1,0},{2,1},{3,2},{4,3},{5,4},{6,5},{7,6},{8,7},{9,8},{10,9},{11,1... | collective-permute-start | bytes 147464 | tf_op jit(solution)/shard_map/ppermute | solution.py:25
  98.9 9.3 %collective-permute-start.14 = (f32[3,8,2,128]{3,1,2,0:T(8,128)S(1)}, f32[3,8,2,128]{3,1,2,0:T(8,128)S(1)}, u32[]{:S(2)}, u32[]{:S(2)}) collective-permute-start(f32[3,8,2,128]{3,1,2,0:T(8,128)S(1)} %get-tuple-element.86), channel_id=1, source_target_pairs={{0,1},{1,2},{2,3},{3,4},{4,5},{5,6},{6,7},{7,8},{8,9},{9,10},{10,1... | collective-permute-start | bytes 73736 | tf_op jit(solution)/shard_map/ppermute | solution.py:22
  100.8 8.8 %collective-permute-start.15 = (f32[3,8,2,128]{3,1,2,0:T(8,128)S(1)}, f32[3,8,2,128]{3,1,2,0:T(8,128)S(1)}, u32[]{:S(2)}, u32[]{:S(2)}) collective-permute-start(f32[3,8,2,128]{3,1,2,0:T(8,128)S(1)} %get-tuple-element.87), channel_id=1, source_target_pairs={{1,0},{2,1},{3,2},{4,3},{5,4},{6,5},{7,6},{8,7},{9,8},{10,9},{11,1... | collective-permute-start | bytes 73736 | tf_op jit(solution)/shard_map/ppermute | solution.py:25
  113.0 8.3 %collective-permute-start.16 = (f32[6,2,12,128]{3,1,2,0:T(2,128)S(1)}, f32[6,2,12,128]{3,1,2,0:T(2,128)S(1)}, u32[]{:S(2)}, u32[]{:S(2)}) collective-permute-start(f32[6,2,12,128]{3,1,2,0:T(2,128)S(1)} %get-tuple-element.85), channel_id=1, source_target_pairs={{128,0},{256,128},{384,256},{512,384},{640,512},{768,640},{896,768... | collective-permute-start | bytes 221192 | tf_op jit(solution)/shard_map/ppermute | solution.py:25
  119.3 8.4 %collective-permute-start.17 = (f32[6,2,12,128]{3,1,2,0:T(2,128)S(1)}, f32[6,2,12,128]{3,1,2,0:T(2,128)S(1)}, u32[]{:S(2)}, u32[]{:S(2)}) collective-permute-start(f32[6,2,12,128]{3,1,2,0:T(2,128)S(1)} %get-tuple-element.84), channel_id=1, source_target_pairs={{0,128},{128,256},{256,384},{384,512},{512,640},{640,768},{768,896... | collective-permute-start | bytes 221192 | tf_op jit(solution)/shard_map/ppermute | solution.py:22
  127.7 9.3 %collective-permute-start.18 = (f32[6,8,2,128]{3,1,2,0:T(8,128)S(1)}, f32[6,8,2,128]{3,1,2,0:T(8,128)S(1)}, u32[]{:S(2)}, u32[]{:S(2)}) collective-permute-start(f32[6,8,2,128]{3,1,2,0:T(8,128)S(1)} %get-tuple-element.60), channel_id=1, source_target_pairs={{0,1},{1,2},{2,3},{3,4},{4,5},{5,6},{6,7},{7,8},{8,9},{9,10},{10,1... | collective-permute-start | bytes 147464 | tf_op jit(solution)/shard_map/ppermute | solution.py:22
  129.7 9.0 %collective-permute-start.19 = (f32[6,8,2,128]{3,1,2,0:T(8,128)S(1)}, f32[6,8,2,128]{3,1,2,0:T(8,128)S(1)}, u32[]{:S(2)}, u32[]{:S(2)}) collective-permute-start(f32[6,8,2,128]{3,1,2,0:T(8,128)S(1)} %get-tuple-element.61), channel_id=1, source_target_pairs={{1,0},{2,1},{3,2},{4,3},{5,4},{6,5},{7,6},{8,7},{9,8},{10,9},{11,1... | collective-permute-start | bytes 147464 | tf_op jit(solution)/shard_map/ppermute | solution.py:25
  148.8 9.3 %collective-permute-start.22 = (f32[3,8,2,128]{3,1,2,0:T(8,128)S(1)}, f32[3,8,2,128]{3,1,2,0:T(8,128)S(1)}, u32[]{:S(2)}, u32[]{:S(2)}) collective-permute-start(f32[3,8,2,128]{3,1,2,0:T(8,128)S(1)} %get-tuple-element.82), channel_id=1, source_target_pairs={{0,1},{1,2},{2,3},{3,4},{4,5},{5,6},{6,7},{7,8},{8,9},{9,10},{10,1... | collective-permute-start | bytes 73736 | tf_op jit(solution)/shard_map/ppermute | solution.py:22
  150.7 8.8 %collective-permute-start.23 = (f32[3,8,2,128]{3,1,2,0:T(8,128)S(1)}, f32[3,8,2,128]{3,1,2,0:T(8,128)S(1)}, u32[]{:S(2)}, u32[]{:S(2)}) collective-permute-start(f32[3,8,2,128]{3,1,2,0:T(8,128)S(1)} %get-tuple-element.83), channel_id=1, source_target_pairs={{1,0},{2,1},{3,2},{4,3},{5,4},{6,5},{7,6},{8,7},{9,8},{10,9},{11,1... | collective-permute-start | bytes 73736 | tf_op jit(solution)/shard_map/ppermute | solution.py:25
  169.2 8.4 %collective-permute-start.25 = (f32[6,2,12,128]{3,1,2,0:T(2,128)S(1)}, f32[6,2,12,128]{3,1,2,0:T(2,128)S(1)}, u32[]{:S(2)}, u32[]{:S(2)}) collective-permute-start(f32[6,2,12,128]{3,1,2,0:T(2,128)S(1)} %get-tuple-element.80), channel_id=1, source_target_pairs={{0,128},{128,256},{256,384},{384,512},{512,640},{640,768},{768,896... | collective-permute-start | bytes 221192 | tf_op jit(solution)/shard_map/ppermute | solution.py:22
  177.6 9.3 %collective-permute-start.26 = (f32[6,8,2,128]{3,1,2,0:T(8,128)S(1)}, f32[6,8,2,128]{3,1,2,0:T(8,128)S(1)}, u32[]{:S(2)}, u32[]{:S(2)}) collective-permute-start(f32[6,8,2,128]{3,1,2,0:T(8,128)S(1)} %get-tuple-element.58), channel_id=1, source_target_pairs={{0,1},{1,2},{2,3},{3,4},{4,5},{5,6},{6,7},{7,8},{8,9},{9,10},{10,1... | collective-permute-start | bytes 147464 | tf_op jit(solution)/shard_map/ppermute | solution.py:22
  179.5 9.0 %collective-permute-start.27 = (f32[6,8,2,128]{3,1,2,0:T(8,128)S(1)}, f32[6,8,2,128]{3,1,2,0:T(8,128)S(1)}, u32[]{:S(2)}, u32[]{:S(2)}) collective-permute-start(f32[6,8,2,128]{3,1,2,0:T(8,128)S(1)} %get-tuple-element.59), channel_id=1, source_target_pairs={{1,0},{2,1},{3,2},{4,3},{5,4},{6,5},{7,6},{8,7},{9,8},{10,9},{11,1... | collective-permute-start | bytes 147464 | tf_op jit(solution)/shard_map/ppermute | solution.py:25
  198.7 9.3 %collective-permute-start.30 = (f32[3,8,2,128]{3,1,2,0:T(8,128)S(1)}, f32[3,8,2,128]{3,1,2,0:T(8,128)S(1)}, u32[]{:S(2)}, u32[]{:S(2)}) collective-permute-start(f32[3,8,2,128]{3,1,2,0:T(8,128)S(1)} %get-tuple-element.78), channel_id=1, source_target_pairs={{0,1},{1,2},{2,3},{3,4},{4,5},{5,6},{6,7},{7,8},{8,9},{9,10},{10,1... | collective-permute-start | bytes 73736 | tf_op jit(solution)/shard_map/ppermute | solution.py:22
  200.6 8.8 %collective-permute-start.31 = (f32[3,8,2,128]{3,1,2,0:T(8,128)S(1)}, f32[3,8,2,128]{3,1,2,0:T(8,128)S(1)}, u32[]{:S(2)}, u32[]{:S(2)}) collective-permute-start(f32[3,8,2,128]{3,1,2,0:T(8,128)S(1)} %get-tuple-element.79), channel_id=1, source_target_pairs={{1,0},{2,1},{3,2},{4,3},{5,4},{6,5},{7,6},{8,7},{9,8},{10,9},{11,1... | collective-permute-start | bytes 73736 | tf_op jit(solution)/shard_map/ppermute | solution.py:25
  (20 other events, 120.8 us)
where the time goes:
time: 216 us; the launch traced here: 214 us
  starting transfers between devices  147 us (68%)
  waiting for transfers between devices  40.9 us (19%)
  other arithmetic  15.9 us (7%)
  local copies, waits for them, and re-layouts  8.06 us (4%)
    ppermute x16, starting transfers between devices, with_halo(): lax.ppermute(lax.slice_in_dim(block, 0, width, axis=dim), axis, backward)  116 us
    ppermute x16, starting transfers between devices, with_halo(): lax.ppermute(lax.slice_in_dim(block, block.shape[dim] - width, None, axis...  30.7 us
    ppermute x16, waiting for transfers between devices, with_halo(): lax.ppermute(lax.slice_in_dim(block, block.shape[dim] - width, None, axis...  24.4 us
    ppermute x16, waiting for transfers between devices, with_halo(): lax.ppermute(lax.slice_in_dim(block, 0, width, axis=dim), axis, backward)  16.5 us
    scatter-add x4, other arithmetic, shards(): flat.at[normal_rows[:, None], source_cells[None, :]]  4.56 us
  transfers between devices with their start and end apart: 32, of which 16 were waited for; matrix products, arithmetic and copies ran while one was open for 1% of the time, Pallas kernels for 0%

commit v1 on v0

v1 whole, which is shorter than its diff:
```python
import functools

import jax
import jax.numpy as jnp
from jax import lax
from jax.experimental import pallas as pl
from jax.experimental.pallas import tpu as pltpu
from jax.sharding import PartitionSpec as P

STEPS = 4
BLK = 4
BLKZ = 32
MESH = pl.DeviceIdType.MESH

inner_coef = 9.0 / 8.0
outer_coef = 1.0 / 24.0
time_step = 0.08
friction = 0.4
log2_e = 1.4426950408889634
ln_2 = 0.6931471805599453

LAYERS = 8
ROWS = 16

TO_HIGH = ((4, 0), (5, 1), (5, 1))
TO_LOW = ((0, 4), (1, 5), (1, 5))


def forward(layers, i):
    return combine(layers, (i + 1, i, i + 2, i - 1))


def backward(layers, i):
    return combine(layers, (i, i - 1, i + 1, i - 2))


def combine(layers, at):
    terms = []
    for index, coef in zip(at, (inner_coef, -inner_coef, -outer_coef, outer_coef)):
        if 0 <= index < len(layers):
            terms.append((coef, layers[index]))
    total = None
    for coef, layer in terms:
        total = coef * layer if total is None else total + coef * layer
    return total


def moved(field, offset, axis):
    size = field.shape[axis]
    return pltpu.roll(field, (-offset) % size, axis)


def forward_rows(field):
    return inner_coef * (moved(field, 1, 1) - field) - outer_coef * (
        moved(field, 2, 1) - moved(field, -1, 1)
    )


def backward_rows(field):
    return inner_coef * (field - moved(field, -1, 1)) - outer_coef * (
        moved(field, 1, 1) - moved(field, -2, 1)
    )


def kernel(
    counts,
    vel_in,
    str_in,
    mem_in,
    code_in,
    scale,
    table,
    cells,
    amps,
    vel_out,
    str_out,
    mem_out,
    V,
    S,
    M,
    CODE,
    G,
    RA,
    RB,
    DB,
    PROP,
    SRC,
    load_sem,
    first_send,
    first_recv,
    send_sem,
    recv_sem,
):
    n_we, n_sn = counts
    we = lax.axis_index("we")
    sn = lax.axis_index("sn")
    east, west = lax.rem(we + 1, n_we), lax.rem(we + n_we - 1, n_we)
    north, south = lax.rem(sn + 1, n_sn), lax.rem(sn + n_sn - 1, n_sn)
    side = {1: east, -1: west}
    along = {1: north, -1: south}
    off_x = {1: jnp.where(we == n_we - 1, 2, 0), -1: jnp.where(we == 0, 2, 0)}
    off_y = {1: jnp.where(sn == n_sn - 1, 2, 0), -1: jnp.where(sn == 0, 2, 0)}

    def to(dx, dy):
        return (
            side[dx] if dx else we,
            along[dy] if dy else sn,
        )

    around = [(dx, dy) for dx in (-1, 0, 1) for dy in (-1, 0, 1) if dx or dy]

    own_v = V.at[:, 2:6, 2:14, :]
    own_s = S.at[:, :, 2:14, :]
    own_m = M.at[:, :, 2:14, :]
    loads = [
        pltpu.make_async_copy(str_in, own_s, load_sem.at[0]),
        pltpu.make_async_copy(code_in, CODE.at[2:6, 2:14, :], load_sem.at[1]),
        pltpu.make_async_copy(vel_in, own_v, load_sem.at[2]),
        pltpu.make_async_copy(mem_in, own_m, load_sem.at[3]),
    ]
    for load in loads:
        load.start()

    zero_slot = jnp.zeros((2, 3, LAYERS, ROWS, 128), jnp.float32)
    RA[0:2] = zero_slot
    RB[0:2] = zero_slot
    edge_rows = jnp.zeros((6, 4, 2, 128), jnp.float32)
    S[:, :, 0:2, :] = edge_rows
    S[:, :, 14:16, :] = edge_rows
    G[0, 7] = jnp.zeros((ROWS, 128), jnp.float32)
    G[1, 0] = jnp.zeros((ROWS, 128), jnp.float32)
    G[2, 0] = jnp.zeros((ROWS, 128), jnp.float32)

    barrier = pltpu.get_barrier_semaphore()
    for dx, dy in around:
        pl.semaphore_signal(barrier, inc=1, device_id=to(dx, dy), device_id_type=MESH)
    pl.semaphore_wait(barrier, len(around))

    first = []

    def send_first(src, dst, dx, dy):
        k = len(first)
        first.append(
            pltpu.make_async_remote_copy(
                src_ref=src,
                dst_ref=dst,
                send_sem=first_send.at[k],
                recv_sem=first_recv.at[k],
                device_id=to(dx, dy),
                device_id_type=MESH,
            )
        )
        first[-1].start()

    send_first(vel_in.at[:, 2:4], V.at[:, 0:2, 2:14, :], 1, 0)
    send_first(vel_in.at[:, 0:2], V.at[:, 6:8, 2:14, :], -1, 0)
    send_first(vel_in.at[:, :, 10:12, :], V.at[:, 2:6, 0:2, :], 0, 1)
    send_first(vel_in.at[:, :, 0:2, :], V.at[:, 2:6, 14:16, :], 0, -1)
    send_first(code_in.at[2:4], CODE.at[0:2, 2:14, :], 1, 0)
    send_first(code_in.at[0:2], CODE.at[6:8, 2:14, :], -1, 0)
    send_first(code_in.at[:, 10:12, :], CODE.at[2:6, 0:2, :], 0, 1)
    send_first(code_in.at[:, 0:2, :], CODE.at[2:6, 14:16, :], 0, -1)

    loads[0].wait()

    block = (4, ROWS, 128)
    lane = lax.broadcasted_iota(jnp.int32, (1, 1, 128), 2)
    row = lax.broadcasted_iota(jnp.int32, (1, ROWS, 128), 1)

    def lane_coef(coef, offset):
        inside = (lane + offset >= 0) & (lane + offset < 128)
        return jnp.where(inside, coef, 0.0)

    def forward_lanes(field):
        return (
            lane_coef(inner_coef, 1) * moved(field, 1, 2)
            - inner_coef * field
            - lane_coef(outer_coef, 2) * moved(field, 2, 2)
            + lane_coef(outer_coef, -1) * moved(field, -1, 2)
        )

    def backward_lanes(field):
        return (
            inner_coef * field
            - lane_coef(inner_coef, -1) * moved(field, -1, 2)
            - lane_coef(outer_coef, 1) * moved(field, 1, 2)
            + lane_coef(outer_coef, -2) * moved(field, -2, 2)
        )

    def force(component, along_x, field_x, rest):
        layers = [field_x[i] for i in range(4)]
        for i in range(-2, 6):
            part = along_x(layers, i)
            if part is None:
                continue
            if 0 <= i < 4:
                part = part + rest[i]
            G[component, i + 2] = part

    def step(t, carry):
        slot = lax.rem(t, 2)
        copies = []

        def send(src, ref, dst, dx, dy):
            k = len(copies)
            there = slot
            if dx and dy:
                there = slot + jnp.maximum(off_x[dx], off_y[dy])
            elif dx:
                there = slot + off_x[dx]
            else:
                there = slot + off_y[dy]
            copies.append(
                pltpu.make_async_remote_copy(
                    src_ref=src,
                    dst_ref=ref.at[(there,) + dst],
                    send_sem=send_sem.at[slot, k],
                    recv_sem=recv_sem.at[slot, k],
                    device_id=to(dx, dy),
                    device_id_type=MESH,
                )
            )
            copies[-1].start()

        def send_x(c):
            for dx, (here, there) in ((1, TO_HIGH[c]), (-1, TO_LOW[c])):
                send(
                    G.at[c, pl.ds(here, 3), pl.ds(2, 12), :],
                    RA,
                    (c, pl.ds(there, 3), pl.ds(2, 12), slice(None)),
                    dx,
                    0,
                )

        sxx, sxz, sxy, syz, syy, szz = (S[c] for c in range(6))
        force(0, forward, sxx, backward_rows(sxy) + backward_lanes(sxz))
        send_x(0)
        force(1, backward, sxy, forward_rows(syy) + backward_lanes(syz))
        send_x(1)
        force(2, backward, sxz, backward_rows(syz) + forward_lanes(szz))
        send_x(2)

        everything = slice(None)
        for dy, (here, there) in ((1, (12, 0)), (-1, (0, 12))):
            send(
                G.at[:, pl.ds(2, 4), pl.ds(here, 4), :],
                RB,
                (everything, pl.ds(2, 4), pl.ds(there, 4), everything),
                0,
                dy,
            )
        for dx in (1, -1):
            for dy in (1, -1):
                from_l, to_l = (6, 2) if dx == 1 else (0, 4)
                from_r, to_r = (12, 0) if dy == 1 else (2, 14)
                send(
                    G.at[:, pl.ds(from_l, 2), pl.ds(from_r, 2), :],
                    RA,
                    (everything, pl.ds(to_l, 2), pl.ds(to_r, 2), everything),
                    dx,
                    dy,
                )
                from_l, to_l = (4, 0) if dx == 1 else (2, 6)
                from_r, to_r = (14, 2) if dy == 1 else (0, 12)
                send(
                    G.at[:, pl.ds(from_l, 2), pl.ds(from_r, 2), :],
                    RB,
                    (everything, pl.ds(to_l, 2), pl.ds(to_r, 2), everything),
                    dx,
                    dy,
                )

        @pl.when(t == 0)
        def _():
            for load in loads[1:]:
                load.wait()
            for copy in first:
                copy.wait()

            def look_up(code, r):
                values = [table[r, k] for k in range(16)]
                for bit in range(4):
                    chosen = (code & (1 << bit)) != 0
                    values = [
                        jnp.where(chosen, values[2 * k + 1], values[2 * k])
                        for k in range(len(values) // 2)
                    ]
                return values[0]

            layer = lax.broadcasted_iota(jnp.int32, (LAYERS, ROWS, 128), 0)
            rows = lax.broadcasted_iota(jnp.int32, (LAYERS, ROWS, 128), 1)
            inside = (
                (layer >= jnp.where(we == 0, 2, 0))
                & (layer < jnp.where(we == n_we - 1, 6, 8))
                & (rows >= jnp.where(sn == 0, 2, 0))
                & (rows < jnp.where(sn == n_sn - 1, 14, 16))
            )
            DB[...] = jnp.where(inside, time_step * look_up(CODE[...], 0), 0.0)
            for c in range(3):
                V[c] = jnp.where(inside, V[c], 0.0)

            moduli = jnp.zeros((1, ROWS, 128), jnp.float32)
            for j in range(3):
                for k in range(128 // BLKZ):
                    here = (
                        (row >= 2 + BLK * j)
                        & (row < 2 + BLK * (j + 1))
                        & (lane >= BLKZ * k)
                        & (lane < BLKZ * (k + 1))
                    )
                    moduli = jnp.where(here, scale[0, j, k], moduli)
            code = CODE[2:6]
            PROP[0] = look_up(code, 1) * moduli
            PROP[1] = look_up(code, 2) * moduli
            decay = look_up(code, 3)
            gain = (1.0 - decay) * look_up(code, 4)
            PROP[2] = decay
            PROP[3] = gain
            PROP[4] = time_step * (1.0 - 0.5 * gain)
            PROP[5] = (0.5 * time_step) * (1.0 + decay)
            PROP[6] = look_up(code, 5)

            cell = (
                (
                    lax.broadcasted_iota(jnp.int32, block, 0) * 12
                    + lax.broadcasted_iota(jnp.int32, block, 1)
                    - 2
                )
                * 128
                + lax.broadcasted_iota(jnp.int32, block, 2)
            )
            for n in range(STEPS):
                added = jnp.zeros(block, jnp.float32)
                for k in range(4):
                    added = added + jnp.where(
                        cell == cells[0, 0, k], time_step * amps[0, 0, k, n], 0.0
                    )
                SRC[n] = added

        for copy in copies:
            copy.wait()

        for c in range(3):
            V[c] = V[c] + DB[...] * (G[c] + RA[slot, c] + RB[slot, c])

        def forward_x(c):
            return inner_coef * (V[c, 3:7] - V[c, 2:6]) - outer_coef * (V[c, 4:8] - V[c, 1:5])

        def backward_x(c):
            return inner_coef * (V[c, 2:6] - V[c, 1:5]) - outer_coef * (V[c, 3:7] - V[c, 0:4])

        ve, vn, vd = (V[c, 2:6] for c in range(3))
        exx = backward_x(0)
        eyy = backward_rows(vn)
        ezz = backward_lanes(vd)
        exz = forward_lanes(ve) + forward_x(2)
        exy = forward_rows(ve) + forward_x(1)
        eyz = forward_lanes(vn) + forward_rows(vd)
        lame, shear = PROP[0], PROP[1]
        volume = lame * (exx + eyy + ezz)
        twice = shear + shear
        rates = (
            volume + twice * exx,
            shear * exz,
            shear * exy,
            shear * eyz,
            volume + twice * eyy,
            volume + twice * ezz,
        )
        trial = []
        for c in range(6):
            memory = M[c]
            M[c] = PROP[2] * memory + PROP[3] * rates[c]
            trial.append(S[c] + PROP[4] * rates[c] - PROP[5] * memory)
        added = SRC[t]
        for c in (0, 4, 5):
            trial[c] = trial[c] + added
        mean = (trial[0] + trial[4] + trial[5]) * (1.0 / 3.0)
        for c in (0, 4, 5):
            trial[c] = trial[c] - mean
        normal = trial[0] * trial[0] + trial[4] * trial[4] + trial[5] * trial[5]
        second = 0.5 * normal + (
            trial[1] * trial[1] + trial[2] * trial[2] + trial[3] * trial[3]
        )
        soft = jnp.maximum(-mean, 0.0) + ln_2 * jnp.log2(1.0 + jnp.exp2(-log2_e * jnp.abs(mean)))
        level = PROP[6] + friction * soft
        scaled = second / (level * level)
        factor = jnp.exp2(-0.25 * jnp.log2(1.0 + scaled * scaled))
        own = (row >= 2) & (row < 14)
        for c in range(6):
            new = factor * trial[c]
            if c in (0, 4, 5):
                new = mean + new
            S[c] = jnp.where(own, new, 0.0)
        return carry

    lax.fori_loop(0, STEPS, step, 0)

    stores = [
        pltpu.make_async_copy(own_v, vel_out, load_sem.at[0]),
        pltpu.make_async_copy(own_s, str_out, load_sem.at[1]),
        pltpu.make_async_copy(own_m, mem_out, load_sem.at[2]),
    ]
    for store in stores:
        store.start()
    for store in stores:
        store.wait()


def solution(mesh):
    counts = (mesh.shape["we"], mesh.shape["sn"])
    f32 = jnp.float32

    def shards(velocity, stress, memory, code, scale, table, cells, amps):
        hbm = pl.BlockSpec(memory_space=pl.ANY)
        smem = pl.BlockSpec(memory_space=pltpu.SMEM)
        return pl.pallas_call(
            functools.partial(kernel, counts),
            out_shape=tuple(
                jax.ShapeDtypeStruct(a.shape, f32) for a in (velocity, stress, memory)
            ),
            in_specs=[hbm] * 4 + [smem] * 4,
            out_specs=(hbm,) * 3,
            scratch_shapes=[
                pltpu.VMEM((3, LAYERS, ROWS, 128), f32),
                pltpu.VMEM((6, 4, ROWS, 128), f32),
                pltpu.VMEM((6, 4, ROWS, 128), f32),
                pltpu.VMEM((LAYERS, ROWS, 128), jnp.int32),
                pltpu.VMEM((3, LAYERS, ROWS, 128), f32),
                pltpu.VMEM((4, 3, LAYERS, ROWS, 128), f32),
                pltpu.VMEM((4, 3, LAYERS, ROWS, 128), f32),
                pltpu.VMEM((LAYERS, ROWS, 128), f32),
                pltpu.VMEM((7, 4, ROWS, 128), f32),
                pltpu.VMEM((STEPS, 4, ROWS, 128), f32),
                pltpu.SemaphoreType.DMA((4,)),
                pltpu.SemaphoreType.DMA((8,)),
                pltpu.SemaphoreType.DMA((8,)),
                pltpu.SemaphoreType.DMA((2, 16)),
                pltpu.SemaphoreType.DMA((2, 16)),
            ],
            compiler_params=pltpu.CompilerParams(
                collective_id=0, has_side_effects=True, vmem_limit_bytes=16 * 1024 * 1024
            ),
        )(velocity, stress, memory, code, scale, table, cells, amps)

    in_specs = (
        P(None, "we", "sn", None),
        P(None, "we", "sn", None),
        P(None, "we", "sn", None),
        P("we", "sn", None),
        P("we", "sn", None),
        P(),
        P("we", "sn", None),
        P("we", "sn", None, None),
    )
    out_specs = (P(None, "we", "sn", None),) * 3
    return jax.shard_map(shards, mesh=mesh, in_specs=in_specs, out_specs=out_specs, check_vma=False)
```

time: 216 us -> 52.8 us (0.24)
  the two profiles are of different devices: /device:TPU:6 before, /device:TPU:1 now
where the time goes in v1:
time: 52.8 us; the launch traced here: 52.5 us
  Pallas kernels  45.8 us (87%)
  local copies, waits for them, and re-layouts  6.05 us (11%)
  between operations  0.68 us (1%)
    pallas_call x1, Pallas kernels, shards(): pl.pallas_call(functools.partial(kernel, counts), out_shape=tuple((jax.Sh...  45.8 us
    unnamed x15, local copies, waits for them, and re-layouts  3.95 us
    pallas_call x3, local copies, waits for them, and re-layouts, shards(): pl.pallas_call(functools.partial(kernel, counts), out_shape=tuple((jax.Sh...  2.1 us

profile of v1, /device:TPU:1, one launch (start us, length us, event | category | flops | bytes accessed | tf_op | source)
XLA Modules:
  0.0 52.5 jit_solution(4045449085209203382)
XLA Ops:
  0.6 0.0 copy-start.3
  0.6 0.7 %copy.15.scale = f32[1,3,4]{2,1,0:T(4,128)S(1)} copy(f32[1,3,4]{2,0,1:T(1,128)} %param.12) | data formatting | bytes 96 | tf_op args[4]
  1.4 0.7 %copy.14.code_in = s32[4,12,128]{2,1,0:T(8,128)S(1)} copy(s32[4,12,128]{2,0,1:T(4,128)} %param.11) | data formatting | bytes 49152 | tf_op args[3]
  2.1 0.9 %copy.11.vel_in = f32[3,4,12,128]{3,2,1,0:T(8,128)S(1)} copy(f32[3,4,12,128]{3,1,2,0:T(4,128)} %param.8) | data formatting | bytes 147456 | tf_op args[0]
  3.0 0.0 copy-done.3
  3.0 0.0 copy-start.4
  3.0 0.9 %copy-done.4 = f32[6,4,12,128]{3,1,2,0:T(4,128)S(1)} copy-done((f32[6,4,12,128]{3,1,2,0:T(4,128)S(1)}, f32[6,4,12,128]{3,1,2,0:T(4,128)}, u32[]{:S(2)}) %copy-start.4) | copy-done | bytes 147480
  3.9 0.0 copy-start
  3.9 0.0 copy-start.1
  3.9 0.0 copy-start.2
  4.0 0.7 %copy-done = f32[6,16]{1,0:T(8,128)S(1)} copy-done((f32[6,16]{1,0:T(8,128)S(1)}, f32[6,16]{1,0:T(8,128)}, u32[]{:S(2)}) %copy-start) | copy-done | bytes 408
  4.6 0.0 copy-done.1
  4.6 0.0 copy-done.2
  4.6 45.8 %shard_map.103 = (f32[3,4,12,128]{3,2,1,0:T(8,128)S(1)}, f32[6,4,12,128]{3,2,1,0:T(8,128)S(1)}, f32[6,4,12,128]{3,2,1,0:T(8,128)S(1)}) custom-call(f32[3,4,12,128]{3,2,1,0:T(8,128)S(1)} %copy.11.vel_in, f32[6,4,12,128]{3,2,1,0:T(8,128)S(1)} %copy.12.str_in, f32[6,4,12,128]{3,2,1,0:T(8,128)S(1)} %copy.13.mem_in, s32[4,12,128]{2,1,0:T(8,128)S(1)} %copy.14.code_in, ...), custom_call_target="tpu_custom_call" | custom-call | tf_op jit(solution)/shard_map/pallas_call | solution.py:417
  50.4 0.7 %copy.16 = f32[3,4,12,128]{3,1,2,0:T(4,128)} copy(f32[3,4,12,128]{3,2,1,0:T(8,128)S(1)} %get-tuple-element.3) | data formatting | bytes 147456 | tf_op jit(solution)/shard_map/pallas_call | solution.py:417
  51.1 0.7 %copy.17 = f32[6,4,12,128]{3,1,2,0:T(4,128)} copy(f32[6,4,12,128]{3,2,1,0:T(8,128)S(1)} %get-tuple-element.4) | data formatting | bytes 294912 | tf_op jit(solution)/shard_map/pallas_call | solution.py:417
  51.8 0.7 %copy.18 = f32[6,4,12,128]{3,1,2,0:T(4,128)} copy(f32[6,4,12,128]{3,2,1,0:T(8,128)S(1)} %get-tuple-element.5) | data formatting | bytes 294912 | tf_op jit(solution)/shard_map/pallas_call | solution.py:417
  (2 shorter events, 0.0 us)
Async XLA Ops:
  0.6 2.4 %copy-start.3 = (f32[6,4,12,128]{3,1,2,0:T(4,128)S(1)}, f32[6,4,12,128]{3,1,2,0:T(4,128)}, u32[]{:S(2)}) copy-start(f32[6,4,12,128]{3,1,2,0:T(4,128)} %param.9) | copy-start | bytes 442372
  3.0 0.9 %copy-start.4 = (f32[6,4,12,128]{3,1,2,0:T(4,128)S(1)}, f32[6,4,12,128]{3,1,2,0:T(4,128)}, u32[]{:S(2)}) copy-start(f32[6,4,12,128]{3,1,2,0:T(4,128)} %param.10) | copy-start | bytes 442372
  3.9 0.7 %copy-start = (f32[6,16]{1,0:T(8,128)S(1)}, f32[6,16]{1,0:T(8,128)}, u32[]{:S(2)}) copy-start(f32[6,16]{1,0:T(8,128)} %table.1) | copy-start | bytes 1156
  3.9 0.7 %copy-start.1 = (f32[1,1,4,4]{3,2,1,0:T(4,128)S(1)}, f32[1,1,4,4]{3,2,1,0:T(4,128)}, u32[]{:S(2)}) copy-start(f32[1,1,4,4]{3,2,1,0:T(4,128)} %amps.1) | copy-start | bytes 196
  3.9 0.7 %copy-start.2 = (s32[1,1,4]{2,1,0:T(1,128)S(1)}, s32[1,1,4]{2,1,0:T(1,128)}, u32[]{:S(2)}) copy-start(s32[1,1,4]{2,1,0:T(1,128)} %cells.1) | copy-start | bytes 52

commit v2 on v1

v2 whole, which is shorter than its diff:
```python
import functools

import jax
import jax.numpy as jnp
from jax import lax
from jax.experimental import pallas as pl
from jax.experimental.pallas import tpu as pltpu
from jax.sharding import PartitionSpec as P

STEPS = 4
BLK = 4
BLKZ = 32
MESH = pl.DeviceIdType.MESH

inner_coef = 9.0 / 8.0
outer_coef = 1.0 / 24.0
time_step = 0.08
friction = 0.4
log2_e = 1.4426950408889634
ln_2 = 0.6931471805599453

LAYERS = 8
ROWS = 16

TO_HIGH = ((4, 0), (5, 1), (5, 1))
TO_LOW = ((0, 4), (1, 5), (1, 5))


def forward(layers, i):
    return combine(layers, (i + 1, i, i + 2, i - 1))


def backward(layers, i):
    return combine(layers, (i, i - 1, i + 1, i - 2))


def combine(layers, at):
    terms = []
    for index, coef in zip(at, (inner_coef, -inner_coef, -outer_coef, outer_coef)):
        if 0 <= index < len(layers):
            terms.append((coef, layers[index]))
    total = None
    for coef, layer in terms:
        total = coef * layer if total is None else total + coef * layer
    return total


def moved(field, offset, axis):
    size = field.shape[axis]
    return pltpu.roll(field, (-offset) % size, axis)


def forward_rows(field):
    return inner_coef * (moved(field, 1, 1) - field) - outer_coef * (
        moved(field, 2, 1) - moved(field, -1, 1)
    )


def backward_rows(field):
    return inner_coef * (field - moved(field, -1, 1)) - outer_coef * (
        moved(field, 1, 1) - moved(field, -2, 1)
    )


def kernel(
    counts,
    vel_in,
    str_in,
    mem_in,
    code_in,
    scale_in,
    table_in,
    cells_in,
    amps_in,
    vel_out,
    str_out,
    mem_out,
    V,
    S,
    M,
    CODE,
    G,
    RA,
    RB,
    DB,
    PROP,
    SRC,
    scale,
    table,
    cells,
    amps,
    load_sem,
    small_sem,
    first_send,
    first_recv,
    send_sem,
    recv_sem,
):
    n_we, n_sn = counts
    we = lax.axis_index("we")
    sn = lax.axis_index("sn")
    side = {
        0: we,
        1: jnp.minimum(we + 1, n_we - 1),
        -1: jnp.maximum(we - 1, 0),
    }
    along = {
        0: sn,
        1: jnp.minimum(sn + 1, n_sn - 1),
        -1: jnp.maximum(sn - 1, 0),
    }
    has_x = {1: we < n_we - 1, -1: we > 0}
    has_y = {1: sn < n_sn - 1, -1: sn > 0}

    def there(dx, dy):
        if dx and dy:
            return has_x[dx] & has_y[dy]
        return has_x[dx] if dx else has_y[dy]

    around = [(dx, dy) for dx in (1, -1) for dy in (1, -1)]
    around += [(0, 1), (0, -1), (1, 0), (-1, 0)]

    RA[0] = jnp.zeros((3, LAYERS, ROWS, 128), jnp.float32)
    RB[0] = jnp.zeros((3, LAYERS, ROWS, 128), jnp.float32)

    barrier = pltpu.get_barrier_semaphore()
    for dx, dy in around:

        @pl.when(there(dx, dy))
        def _():
            pl.semaphore_signal(
                barrier, inc=1, device_id=(side[dx], along[dy]), device_id_type=MESH
            )

    loads = []
    for n, (src, dst, first) in enumerate(((str_in, S, 0), (code_in, CODE, 2), (vel_in, V, 2), (mem_in, M, 0))):
        for x in range(4):
            if src is code_in:
                pair = src.at[:, x, :], dst.at[first + x, 2:14, :]
            else:
                pair = src.at[:, :, x, :], dst.at[:, first + x, 2:14, :]
            loads.append(pltpu.make_async_copy(*pair, load_sem.at[n, x]))
            loads[-1].start()
    small = [
        pltpu.make_async_copy(src, dst, small_sem.at[n])
        for n, (src, dst) in enumerate(
            ((scale_in, scale), (table_in, table), (cells_in, cells), (amps_in, amps))
        )
    ]
    for load in small:
        load.start()

    edge_rows = jnp.zeros((6, 4, 2, 128), jnp.float32)
    S[:, :, 0:2, :] = edge_rows
    S[:, :, 14:16, :] = edge_rows
    G[0, 7] = jnp.zeros((ROWS, 128), jnp.float32)
    G[1, 0] = jnp.zeros((ROWS, 128), jnp.float32)
    G[2, 0] = jnp.zeros((ROWS, 128), jnp.float32)
    RA[1] = jnp.zeros((3, LAYERS, ROWS, 128), jnp.float32)
    RB[1] = jnp.zeros((3, LAYERS, ROWS, 128), jnp.float32)

    block = (4, ROWS, 128)
    lane = lax.broadcasted_iota(jnp.int32, (1, 1, 128), 2)
    row = lax.broadcasted_iota(jnp.int32, (1, ROWS, 128), 1)

    def lane_coef(coef, offset):
        inside = (lane + offset >= 0) & (lane + offset < 128)
        return jnp.where(inside, coef, 0.0)

    def forward_lanes(field):
        return (
            lane_coef(inner_coef, 1) * moved(field, 1, 2)
            - inner_coef * field
            - lane_coef(outer_coef, 2) * moved(field, 2, 2)
            + lane_coef(outer_coef, -1) * moved(field, -1, 2)
        )

    def backward_lanes(field):
        return (
            inner_coef * field
            - lane_coef(inner_coef, -1) * moved(field, -1, 2)
            - lane_coef(outer_coef, 1) * moved(field, 1, 2)
            + lane_coef(outer_coef, -2) * moved(field, -2, 2)
        )

    def force(component, along_x, field_x, rest):
        layers = [field_x[i] for i in range(4)]
        for i in range(-2, 6):
            part = along_x(layers, i)
            if part is None:
                continue
            if 0 <= i < 4:
                part = part + rest[i]
            G[component, i + 2] = part

    def forces():
        sxx, sxz, sxy, syz, syy, szz = (S[c] for c in range(6))
        force(0, forward, sxx, backward_rows(sxy) + backward_lanes(sxz))
        force(1, backward, sxy, forward_rows(syy) + backward_lanes(syz))
        force(2, backward, sxz, backward_rows(syz) + forward_lanes(szz))

    everything = slice(None)

    def first_copies(dx, dy):
        if dx and dy:
            return []
        k = {(1, 0): 0, (-1, 0): 1, (0, 1): 2, (0, -1): 3}[dx, dy]
        here, into = {
            (1, 0): ((pl.ds(4, 2), pl.ds(2, 12)), (pl.ds(0, 2), pl.ds(2, 12))),
            (-1, 0): ((pl.ds(2, 2), pl.ds(2, 12)), (pl.ds(6, 2), pl.ds(2, 12))),
            (0, 1): ((pl.ds(2, 4), pl.ds(12, 2)), (pl.ds(2, 4), pl.ds(0, 2))),
            (0, -1): ((pl.ds(2, 4), pl.ds(2, 2)), (pl.ds(2, 4), pl.ds(14, 2))),
        }[dx, dy]
        pairs = [
            (V.at[(everything,) + here], V.at[(everything,) + into]),
            (CODE.at[here], CODE.at[into]),
        ]
        return [
            pltpu.make_async_remote_copy(
                src_ref=src,
                dst_ref=dst,
                send_sem=first_send.at[k, n],
                recv_sem=first_recv.at[k, n],
                device_id=(side[dx], along[dy]),
                device_id_type=MESH,
            )
            for n, (src, dst) in enumerate(pairs)
        ]

    def step_copies(t, dx, dy):
        slot = lax.rem(t, 2)
        plan = []
        if dx and dy:
            from_l, to_l = (6, 2) if dx == 1 else (0, 4)
            from_r, to_r = (12, 0) if dy == 1 else (2, 14)
            plan.append((everything, from_l, 2, from_r, 2, RA, to_l, to_r))
            from_l, to_l = (4, 0) if dx == 1 else (2, 6)
            from_r, to_r = (14, 2) if dy == 1 else (0, 12)
            plan.append((everything, from_l, 2, from_r, 2, RB, to_l, to_r))
        elif dy:
            from_r, to_r = (12, 0) if dy == 1 else (0, 12)
            plan.append((everything, 2, 4, from_r, 4, RB, 2, to_r))
        else:
            for c in range(3):
                from_l, to_l = (TO_HIGH if dx == 1 else TO_LOW)[c]
                plan.append((c, from_l, 3, 2, 12, RA, to_l, 2))
        k = around.index((dx, dy))
        return [
            pltpu.make_async_remote_copy(
                src_ref=G.at[c, pl.ds(from_l, n_l), pl.ds(from_r, n_r), :],
                dst_ref=ref.at[slot, c, pl.ds(to_l, n_l), pl.ds(to_r, n_r), :],
                send_sem=send_sem.at[slot, k, n],
                recv_sem=recv_sem.at[slot, k, n],
                device_id=(side[dx], along[dy]),
                device_id_type=MESH,
            )
            for n, (c, from_l, n_l, from_r, n_r, ref, to_l, to_r) in enumerate(plan)
        ]

    def start_all(copies_of):
        for dx, dy in around:

            @pl.when(there(dx, dy))
            def _():
                for copy in copies_of(dx, dy):
                    copy.start()

    def wait_all(copies_of, received):
        for dx, dy in around:

            @pl.when(there(-dx, -dy) if received else there(dx, dy))
            def _():
                for copy in copies_of(dx, dy):
                    if received:
                        copy.wait_recv()
                    else:
                        copy.wait_send()

    for load in loads[:4]:
        load.wait()
    forces()
    for load in loads[4:]:
        load.wait()

    n_x = 1 + has_x[1].astype(jnp.int32) + has_x[-1].astype(jnp.int32)
    n_y = 1 + has_y[1].astype(jnp.int32) + has_y[-1].astype(jnp.int32)
    pl.semaphore_wait(barrier, n_x * n_y - 1)
    start_all(functools.partial(step_copies, 0))
    start_all(first_copies)
    for load in small:
        load.wait()

    def look_up(code, r):
        values = [table[r, k] for k in range(16)]
        for bit in range(4):
            chosen = (code & (1 << bit)) != 0
            values = [
                jnp.where(chosen, values[2 * k + 1], values[2 * k])
                for k in range(len(values) // 2)
            ]
        return values[0]

    moduli = jnp.zeros((1, ROWS, 128), jnp.float32)
    for j in range(3):
        for k in range(128 // BLKZ):
            here = (
                (row >= 2 + BLK * j)
                & (row < 2 + BLK * (j + 1))
                & (lane >= BLKZ * k)
                & (lane < BLKZ * (k + 1))
            )
            moduli = jnp.where(here, scale[j, 0, k], moduli)
    code = CODE[2:6, 2:14]

    def keep(n, value):
        PROP[n, :, 2:14] = value

    own_moduli = moduli[:, 2:14]
    keep(0, look_up(code, 1) * own_moduli)
    keep(1, look_up(code, 2) * own_moduli)
    decay = look_up(code, 3)
    gain = (1.0 - decay) * look_up(code, 4)
    keep(2, decay)
    keep(3, gain)
    keep(4, time_step * (1.0 - 0.5 * gain))
    keep(5, (0.5 * time_step) * (1.0 + decay))
    keep(6, look_up(code, 5))

    cell = (
        (
            lax.broadcasted_iota(jnp.int32, block, 0) * 12
            + lax.broadcasted_iota(jnp.int32, block, 1)
            - 2
        )
        * 128
        + lax.broadcasted_iota(jnp.int32, block, 2)
    )
    for n in range(STEPS):
        added = jnp.zeros(block, jnp.float32)
        for k in range(4):
            added = added + jnp.where(
                cell == cells[0, 0, k], time_step * amps[0, 0, k, n], 0.0
            )
        SRC[n] = added

    wait_all(first_copies, True)
    wait_all(first_copies, False)

    layer = lax.broadcasted_iota(jnp.int32, (LAYERS, ROWS, 128), 0)
    rows = lax.broadcasted_iota(jnp.int32, (LAYERS, ROWS, 128), 1)
    inside = (
        (layer >= jnp.where(we == 0, 2, 0))
        & (layer < jnp.where(we == n_we - 1, 6, 8))
        & (rows >= jnp.where(sn == 0, 2, 0))
        & (rows < jnp.where(sn == n_sn - 1, 14, 16))
    )
    DB[...] = jnp.where(inside, time_step * look_up(CODE[...], 0), 0.0)
    for c in range(3):
        V[c] = jnp.where(inside, V[c], 0.0)

    v_stores = [
        pltpu.make_async_copy(V.at[:, 2 + x, 2:14, :], vel_out.at[:, :, x, :], load_sem.at[0, x])
        for x in range(4)
    ]

    def step(t, carry):
        copies = functools.partial(step_copies, t)
        slot = lax.rem(t, 2)
        wait_all(copies, True)

        for c in range(3):
            V[c] = V[c] + DB[...] * (G[c] + RA[slot, c] + RB[slot, c])

        @pl.when(t == STEPS - 1)
        def _():
            for store in v_stores:
                store.start()

        def forward_x(c):
            return inner_coef * (V[c, 3:7] - V[c, 2:6]) - outer_coef * (V[c, 4:8] - V[c, 1:5])

        def backward_x(c):
            return inner_coef * (V[c, 2:6] - V[c, 1:5]) - outer_coef * (V[c, 3:7] - V[c, 0:4])

        ve, vn, vd = (V[c, 2:6] for c in range(3))
        exx = backward_x(0)
        eyy = backward_rows(vn)
        ezz = backward_lanes(vd)
        exz = forward_lanes(ve) + forward_x(2)
        exy = forward_rows(ve) + forward_x(1)
        eyz = forward_lanes(vn) + forward_rows(vd)
        lame, shear = PROP[0], PROP[1]
        volume = lame * (exx + eyy + ezz)
        twice = shear + shear
        rates = (
            volume + twice * exx,
            shear * exz,
            shear * exy,
            shear * eyz,
            volume + twice * eyy,
            volume + twice * ezz,
        )
        trial = []
        for c in range(6):
            memory = M[c]
            M[c] = PROP[2] * memory + PROP[3] * rates[c]
            trial.append(S[c] + PROP[4] * rates[c] - PROP[5] * memory)
        added = SRC[t]
        for c in (0, 4, 5):
            trial[c] = trial[c] + added
        mean = (trial[0] + trial[4] + trial[5]) * (1.0 / 3.0)
        for c in (0, 4, 5):
            trial[c] = trial[c] - mean
        normal = trial[0] * trial[0] + trial[4] * trial[4] + trial[5] * trial[5]
        second = 0.5 * normal + (
            trial[1] * trial[1] + trial[2] * trial[2] + trial[3] * trial[3]
        )
        soft = jnp.maximum(-mean, 0.0) + ln_2 * jnp.log2(1.0 + jnp.exp2(-log2_e * jnp.abs(mean)))
        level = PROP[6] + friction * soft
        scaled = second / (level * level)
        factor = jnp.exp2(-0.25 * jnp.log2(1.0 + scaled * scaled))
        own = (row >= 2) & (row < 14)
        for c in range(6):
            new = factor * trial[c]
            if c in (0, 4, 5):
                new = mean + new
            S[c] = jnp.where(own, new, 0.0)

        wait_all(copies, False)

        @pl.when(t < STEPS - 1)
        def _():
            forces()
            start_all(functools.partial(step_copies, t + 1))

        return carry

    lax.fori_loop(0, STEPS, step, 0)

    stores = []
    for n, (src, dst) in enumerate(((S, str_out), (M, mem_out))):
        for x in range(4):
            stores.append(
                pltpu.make_async_copy(
                    src.at[:, x, 2:14, :], dst.at[:, :, x, :], load_sem.at[n + 1, x]
                )
            )
            stores[-1].start()
    for store in v_stores + stores:
        store.wait()


def solution(mesh):
    counts = (mesh.shape["we"], mesh.shape["sn"])
    f32 = jnp.float32

    def shards(velocity, stress, memory, code, scale, table, cells, amps):
        velocity, stress, memory = (
            jnp.transpose(a, (0, 2, 1, 3)) for a in (velocity, stress, memory)
        )
        code = jnp.transpose(code, (1, 0, 2))
        scale = jnp.transpose(scale, (1, 0, 2))
        hbm = pl.BlockSpec(memory_space=pltpu.HBM)
        outs = pl.pallas_call(
            functools.partial(kernel, counts),
            out_shape=tuple(
                jax.ShapeDtypeStruct(a.shape, f32) for a in (velocity, stress, memory)
            ),
            in_specs=[hbm] * 8,
            out_specs=(hbm,) * 3,
            scratch_shapes=[
                pltpu.VMEM((3, LAYERS, ROWS, 128), f32),
                pltpu.VMEM((6, 4, ROWS, 128), f32),
                pltpu.VMEM((6, 4, ROWS, 128), f32),
                pltpu.VMEM((LAYERS, ROWS, 128), jnp.int32),
                pltpu.VMEM((3, LAYERS, ROWS, 128), f32),
                pltpu.VMEM((2, 3, LAYERS, ROWS, 128), f32),
                pltpu.VMEM((2, 3, LAYERS, ROWS, 128), f32),
                pltpu.VMEM((LAYERS, ROWS, 128), f32),
                pltpu.VMEM((7, 4, ROWS, 128), f32),
                pltpu.VMEM((STEPS, 4, ROWS, 128), f32),
                pltpu.SMEM(scale.shape, f32),
                pltpu.SMEM(table.shape, f32),
                pltpu.SMEM(cells.shape, jnp.int32),
                pltpu.SMEM(amps.shape, f32),
                pltpu.SemaphoreType.DMA((4, 4)),
                pltpu.SemaphoreType.DMA((4,)),
                pltpu.SemaphoreType.DMA((4, 2)),
                pltpu.SemaphoreType.DMA((4, 2)),
                pltpu.SemaphoreType.DMA((2, 8, 3)),
                pltpu.SemaphoreType.DMA((2, 8, 3)),
            ],
            compiler_params=pltpu.CompilerParams(
                collective_id=0, has_side_effects=True, vmem_limit_bytes=62 * 1024 * 1024
            ),
        )(velocity, stress, memory, code, scale, table, cells, amps)
        return tuple(jnp.transpose(a, (0, 2, 1, 3)) for a in outs)

    in_specs = (
        P(None, "we", "sn", None),
        P(None, "we", "sn", None),
        P(None, "we", "sn", None),
        P("we", "sn", None),
        P("we", "sn", None),
        P(),
        P("we", "sn", None),
        P("we", "sn", None, None),
    )
    out_specs = (P(None, "we", "sn", None),) * 3
    return jax.shard_map(shards, mesh=mesh, in_specs=in_specs, out_specs=out_specs, check_vma=False)
```

time: 52.8 us -> 47.4 us (0.90)
  the two profiles are of different devices: /device:TPU:1 before, /device:TPU:6 now
where the time goes in v2:
time: 47.4 us; the launch traced here: 47.1 us
  Pallas kernels  43.3 us (91%)
  local copies, waits for them, and re-layouts  3.19 us (7%)
  between operations  0.65 us (1%)
    pallas_call x1, Pallas kernels, shards(): pl.pallas_call(functools.partial(kernel, counts), out_shape=tuple((jax.Sh...  43.3 us
    unnamed x7, local copies, waits for them, and re-layouts  3.19 us

profile of v2, /device:TPU:6, one launch (start us, length us, event | category | flops | bytes accessed | tf_op | source)
XLA Modules:
  0.0 47.1 jit_solution(1330454397555310962)
XLA Ops:
  0.6 43.3 %shard_map.103 = (f32[3,12,4,128]{3,2,1,0:T(4,128)}, f32[6,12,4,128]{3,2,1,0:T(4,128)}, f32[6,12,4,128]{3,2,1,0:T(4,128)}) custom-call(f32[3,12,4,128]{3,2,1,0:T(4,128)} %bitcast.13, f32[6,12,4,128]{3,2,1,0:T(4,128)} %bitcast.8, f32[6,12,4,128]{3,2,1,0:T(4,128)} %bitcast.9, s32[12,4,128]{2,1,0:T(4,128)} %bitcast.14, f32[3,1,4]{2,1,0:T(1,128)} %bitcast.15, ...), custom_call_target="tpu_custom_call" | custom-call | tf_op jit(solution)/shard_map/pallas_call | solution.py:464
  43.9 0.0 copy-start.1
  43.9 1.6 %copy.14 = f32[3,4,12,128]{3,1,2,0:T(4,128)} copy(f32[3,4,12,128]{3,1,2,0:T(4,128)} %bitcast.12) | data formatting | bytes 147456
  45.5 0.0 copy-done.1
  45.5 0.0 copy-start
  45.5 0.7 %copy.15 = f32[6,4,12,128]{3,1,2,0:T(4,128)} copy(f32[6,4,12,128]{3,1,2,0:T(4,128)S(1)} %bitcast.11) | data formatting | bytes 294912
  46.2 0.3 copy-done
  46.5 0.7 %copy.16 = f32[6,4,12,128]{3,1,2,0:T(4,128)} copy(f32[6,4,12,128]{3,1,2,0:T(4,128)S(1)} %bitcast.10) | data formatting | bytes 294912
Async XLA Ops:
  43.9 1.6 %copy-start.1 = (f32[6,12,4,128]{3,2,1,0:T(4,128)S(1)}, f32[6,12,4,128]{3,2,1,0:T(4,128)}, u32[]{:S(2)}) copy-start(f32[6,12,4,128]{3,2,1,0:T(4,128)} %get-tuple-element.7) | copy-start | bytes 442372
  45.5 1.0 %copy-start = (f32[6,12,4,128]{3,2,1,0:T(4,128)S(1)}, f32[6,12,4,128]{3,2,1,0:T(4,128)}, u32[]{:S(2)}) copy-start(f32[6,12,4,128]{3,2,1,0:T(4,128)} %get-tuple-element.8) | copy-start | bytes 442372

commit v3 on v2

--- a/solution.py
+++ b/solution.py
@@ -72,9 +72,6 @@
     table_in,
     cells_in,
     amps_in,
-    vel_out,
-    str_out,
-    mem_out,
     V,
     S,
     M,
@@ -358,11 +355,6 @@
     for c in range(3):
         V[c] = jnp.where(inside, V[c], 0.0)
 
-    v_stores = [
-        pltpu.make_async_copy(V.at[:, 2 + x, 2:14, :], vel_out.at[:, :, x, :], load_sem.at[0, x])
-        for x in range(4)
-    ]
-
     def step(t, carry):
         copies = functools.partial(step_copies, t)
         slot = lax.rem(t, 2)
@@ -370,11 +362,6 @@
 
         for c in range(3):
             V[c] = V[c] + DB[...] * (G[c] + RA[slot, c] + RB[slot, c])
-
-        @pl.when(t == STEPS - 1)
-        def _():
-            for store in v_stores:
-                store.start()
 
         def forward_x(c):
             return inner_coef * (V[c, 3:7] - V[c, 2:6]) - outer_coef * (V[c, 4:8] - V[c, 1:5])
@@ -437,16 +424,18 @@
 
     lax.fori_loop(0, STEPS, step, 0)
 
+
+def write_out(V, S, M, vel_out, str_out, mem_out, sem):
     stores = []
-    for n, (src, dst) in enumerate(((S, str_out), (M, mem_out))):
+    for n, (src, first, dst) in enumerate(((V, 2, vel_out), (S, 0, str_out), (M, 0, mem_out))):
         for x in range(4):
             stores.append(
                 pltpu.make_async_copy(
-                    src.at[:, x, 2:14, :], dst.at[:, :, x, :], load_sem.at[n + 1, x]
+                    src.at[:, first + x, pl.ds(2, 12), :], dst.at[:, :, x, :], sem.at[n, x]
                 )
             )
             stores[-1].start()
-    for store in v_stores + stores:
+    for store in stores:
         store.wait()
 
 
@@ -461,17 +450,21 @@
         code = jnp.transpose(code, (1, 0, 2))
         scale = jnp.transpose(scale, (1, 0, 2))
         hbm = pl.BlockSpec(memory_space=pltpu.HBM)
-        outs = pl.pallas_call(
+        operands = [
+            pltpu.with_memory_space_constraint(a, pltpu.HBM)
+            for a in (velocity, stress, memory, code, scale, table, cells, amps)
+        ]
+        vmem = pl.BlockSpec(memory_space=pltpu.VMEM)
+        fields = pl.pallas_call(
             functools.partial(kernel, counts),
-            out_shape=tuple(
-                jax.ShapeDtypeStruct(a.shape, f32) for a in (velocity, stress, memory)
-            ),
-            in_specs=[hbm] * 8,
-            out_specs=(hbm,) * 3,
-            scratch_shapes=[
+            out_shape=(
                 pltpu.VMEM((3, LAYERS, ROWS, 128), f32),
                 pltpu.VMEM((6, 4, ROWS, 128), f32),
                 pltpu.VMEM((6, 4, ROWS, 128), f32),
+            ),
+            in_specs=[hbm] * 8,
+            out_specs=(vmem,) * 3,
+            scratch_shapes=[
                 pltpu.VMEM((LAYERS, ROWS, 128), jnp.int32),
                 pltpu.VMEM((3, LAYERS, ROWS, 128), f32),
                 pltpu.VMEM((2, 3, LAYERS, ROWS, 128), f32),
@@ -491,9 +484,19 @@
                 pltpu.SemaphoreType.DMA((2, 8, 3)),
             ],
             compiler_params=pltpu.CompilerParams(
-                collective_id=0, has_side_effects=True, vmem_limit_bytes=62 * 1024 * 1024
+                collective_id=0, has_side_effects=True, vmem_limit_bytes=16 * 1024 * 1024
             ),
-        )(velocity, stress, memory, code, scale, table, cells, amps)
+        )(*operands)
+        outs = pl.pallas_call(
+            write_out,
+            out_shape=tuple(
+                jax.ShapeDtypeStruct(a.shape, f32) for a in (velocity, stress, memory)
+            ),
+            in_specs=[vmem] * 3,
+            out_specs=(hbm,) * 3,
+            scratch_shapes=[pltpu.SemaphoreType.DMA((3, 4))],
+            compiler_params=pltpu.CompilerParams(vmem_limit_bytes=4 * 1024 * 1024),
+        )(*(pltpu.with_memory_space_constraint(a, pltpu.VMEM) for a in fields))
         return tuple(jnp.transpose(a, (0, 2, 1, 3)) for a in outs)
 
     in_specs = (

time: 47.4 us -> 44.2 us (0.932)
  local copies, waits for them, and re-layouts: 3.19 us -> 0 us
    unnamed x7 -> x0, local copies, waits for them, and re-layouts: 3.19 us -> none
    pallas_call x1 -> x2, Pallas kernels: 43.3 us -> 43.3 us  [the longest x1 42.5 us: shards(): pl.pallas_call(functools.partial(kernel, counts), out_shape=(pltpu.VMEM((...]
where the time goes in v3:
time: 44.2 us; the launch traced here: 43.9 us
  Pallas kernels  43.3 us (98%)
  between operations  0.64 us (1%)
    pallas_call x1, Pallas kernels, shards(): pl.pallas_call(functools.partial(kernel, counts), out_shape=(pltpu.VMEM((...  42.5 us

profile of v3, /device:TPU:6, one launch (start us, length us, event | category | flops | bytes accessed | tf_op | source)
XLA Modules:
  0.0 43.9 jit_solution(327329692710170200)
XLA Ops:
  0.6 42.5 %shard_map.103 = (f32[3,8,16,128]{3,2,1,0:T(8,128)S(1)}, f32[6,4,16,128]{3,2,1,0:T(8,128)S(1)}, f32[6,4,16,128]{3,2,1,0:T(8,128)S(1)}) custom-call(f32[3,12,4,128]{3,2,1,0:T(4,128)} %bitcast.10, f32[6,12,4,128]{3,2,1,0:T(4,128)} %bitcast.8, f32[6,12,4,128]{3,2,1,0:T(4,128)} %bitcast.9, s32[12,4,128]{2,1,0:T(4,128)} %bitcast.11, f32[3,1,4]{2,1,0:T(1,128)} %bitcast.12, ...), custom_call_target="tpu_custom_call" | custom-call | tf_op jit(solution)/shard_map/pallas_call | solution.py:458
  43.1 0.8 %shard_map.104 = (f32[3,12,4,128]{3,2,1,0:T(4,128)}, f32[6,12,4,128]{3,2,1,0:T(4,128)}, f32[6,12,4,128]{3,2,1,0:T(4,128)}) custom-call(f32[3,8,16,128]{3,2,1,0:T(8,128)S(1)} %get-tuple-element.9.V, f32[6,4,16,128]{3,2,1,0:T(8,128)S(1)} %get-tuple-element.10.S, f32[6,4,16,128]{3,2,1,0:T(8,128)S(1)} %get-tuple-element.11.M), custom_call_target="tpu_custom_call" | custom-call | tf_op jit(solution)/shard_map/pallas_call | solution.py:490

commit v4 on v3

--- a/solution.py
+++ b/solution.py
@@ -77,6 +77,7 @@
     M,
     CODE,
     G,
+    GY,
     RA,
     RB,
     DB,
@@ -101,7 +102,7 @@
         1: jnp.minimum(we + 1, n_we - 1),
         -1: jnp.maximum(we - 1, 0),
     }
-    along = {
+    along_sn = {
         0: sn,
         1: jnp.minimum(sn + 1, n_sn - 1),
         -1: jnp.maximum(sn - 1, 0),
@@ -126,7 +127,7 @@
         @pl.when(there(dx, dy))
         def _():
             pl.semaphore_signal(
-                barrier, inc=1, device_id=(side[dx], along[dy]), device_id_type=MESH
+                barrier, inc=1, device_id=(side[dx], along_sn[dy]), device_id_type=MESH
             )
 
     loads = []
@@ -180,21 +181,28 @@
             + lane_coef(outer_coef, -2) * moved(field, -2, 2)
         )
 
-    def force(component, along_x, field_x, rest):
-        layers = [field_x[i] for i in range(4)]
-        for i in range(-2, 6):
-            part = along_x(layers, i)
-            if part is None:
-                continue
-            if 0 <= i < 4:
-                part = part + rest[i]
-            G[component, i + 2] = part
-
-    def forces():
-        sxx, sxz, sxy, syz, syy, szz = (S[c] for c in range(6))
-        force(0, forward, sxx, backward_rows(sxy) + backward_lanes(sxz))
-        force(1, backward, sxy, forward_rows(syy) + backward_lanes(syz))
-        force(2, backward, sxz, backward_rows(syz) + forward_lanes(szz))
+    along = (forward, backward, backward)
+    along_field = (0, 2, 1)
+
+    def rim_forces():
+        sxy, syz, syy = S[2], S[3], S[4]
+        GY[0] = backward_rows(sxy)
+        GY[1] = forward_rows(syy)
+        GY[2] = backward_rows(syz)
+        for c in range(3):
+            layers = [S[along_field[c], x] for x in range(4)]
+            for i in (-2, -1, 4, 5):
+                part = along[c](layers, i)
+                if part is not None:
+                    G[c, i + 2] = part
+
+    def own_forces():
+        depth = (backward_lanes(S[1]), backward_lanes(S[3]), forward_lanes(S[5]))
+        for c in range(3):
+            layers = [S[along_field[c], x] for x in range(4)]
+            rest = GY[c] + depth[c]
+            for i in range(4):
+                G[c, i + 2] = along[c](layers, i) + rest[i]
 
     everything = slice(None)
 
@@ -218,7 +226,7 @@
                 dst_ref=dst,
                 send_sem=first_send.at[k, n],
                 recv_sem=first_recv.at[k, n],
-                device_id=(side[dx], along[dy]),
+                device_id=(side[dx], along_sn[dy]),
                 device_id_type=MESH,
             )
             for n, (src, dst) in enumerate(pairs)
@@ -230,40 +238,42 @@
         if dx and dy:
             from_l, to_l = (6, 2) if dx == 1 else (0, 4)
             from_r, to_r = (12, 0) if dy == 1 else (2, 14)
-            plan.append((everything, from_l, 2, from_r, 2, RA, to_l, to_r))
-            from_l, to_l = (4, 0) if dx == 1 else (2, 6)
+            plan.append((G, everything, from_l, 2, from_r, 2, RA, to_l, to_r))
+            from_l, to_l = (2, 0) if dx == 1 else (0, 6)
             from_r, to_r = (14, 2) if dy == 1 else (0, 12)
-            plan.append((everything, from_l, 2, from_r, 2, RB, to_l, to_r))
+            plan.append((GY, everything, from_l, 2, from_r, 2, RB, to_l, to_r))
         elif dy:
             from_r, to_r = (12, 0) if dy == 1 else (0, 12)
-            plan.append((everything, 2, 4, from_r, 4, RB, 2, to_r))
+            plan.append((G, everything, 2, 4, from_r, 4, RB, 2, to_r))
         else:
             for c in range(3):
                 from_l, to_l = (TO_HIGH if dx == 1 else TO_LOW)[c]
-                plan.append((c, from_l, 3, 2, 12, RA, to_l, 2))
+                plan.append((G, c, from_l, 3, 2, 12, RA, to_l, 2))
         k = around.index((dx, dy))
         return [
             pltpu.make_async_remote_copy(
-                src_ref=G.at[c, pl.ds(from_l, n_l), pl.ds(from_r, n_r), :],
+                src_ref=field.at[c, pl.ds(from_l, n_l), pl.ds(from_r, n_r), :],
                 dst_ref=ref.at[slot, c, pl.ds(to_l, n_l), pl.ds(to_r, n_r), :],
                 send_sem=send_sem.at[slot, k, n],
                 recv_sem=recv_sem.at[slot, k, n],
-                device_id=(side[dx], along[dy]),
+                device_id=(side[dx], along_sn[dy]),
                 device_id_type=MESH,
             )
-            for n, (c, from_l, n_l, from_r, n_r, ref, to_l, to_r) in enumerate(plan)
+            for n, (field, c, from_l, n_l, from_r, n_r, ref, to_l, to_r) in enumerate(plan)
         ]
 
-    def start_all(copies_of):
-        for dx, dy in around:
+    diagonal, sides = around[:4], around[4:]
+
+    def start_all(copies_of, which):
+        for dx, dy in which:
 
             @pl.when(there(dx, dy))
             def _():
                 for copy in copies_of(dx, dy):
                     copy.start()
 
-    def wait_all(copies_of, received):
-        for dx, dy in around:
+    def wait_all(copies_of, which, received):
+        for dx, dy in which:
 
             @pl.when(there(-dx, -dy) if received else there(dx, dy))
             def _():
@@ -275,15 +285,16 @@
 
     for load in loads[:4]:
         load.wait()
-    forces()
+    rim_forces()
+    own_forces()
     for load in loads[4:]:
         load.wait()
 
     n_x = 1 + has_x[1].astype(jnp.int32) + has_x[-1].astype(jnp.int32)
     n_y = 1 + has_y[1].astype(jnp.int32) + has_y[-1].astype(jnp.int32)
     pl.semaphore_wait(barrier, n_x * n_y - 1)
-    start_all(functools.partial(step_copies, 0))
-    start_all(first_copies)
+    start_all(functools.partial(step_copies, 0), around)
+    start_all(first_copies, sides)
     for load in small:
         load.wait()
 
@@ -340,8 +351,8 @@
             )
         SRC[n] = added
 
-    wait_all(first_copies, True)
-    wait_all(first_copies, False)
+    wait_all(first_copies, sides, True)
+    wait_all(first_copies, sides, False)
 
     layer = lax.broadcasted_iota(jnp.int32, (LAYERS, ROWS, 128), 0)
     rows = lax.broadcasted_iota(jnp.int32, (LAYERS, ROWS, 128), 1)
@@ -358,10 +369,26 @@
     def step(t, carry):
         copies = functools.partial(step_copies, t)
         slot = lax.rem(t, 2)
-        wait_all(copies, True)
-
+
+        def advance(c, layers, rows):
+            at = (layers, rows)
+            arrived = RA[(slot, c) + at] + RB[(slot, c) + at]
+            V[(c,) + at] = V[(c,) + at] + DB[at] * (G[(c,) + at] + arrived)
+
+        wait_all(copies, sides, True)
         for c in range(3):
-            V[c] = V[c] + DB[...] * (G[c] + RA[slot, c] + RB[slot, c])
+            advance(c, slice(2, 6), slice(2, 14))
+        depth_of = (
+            forward_lanes(V[0, 2:6]),
+            forward_lanes(V[1, 2:6]),
+            backward_lanes(V[2, 2:6]),
+        )
+        wait_all(copies, diagonal, True)
+        for c in range(3):
+            advance(c, slice(2, 6), slice(0, 2))
+            advance(c, slice(2, 6), slice(14, 16))
+            advance(c, slice(0, 2), slice(0, 16))
+            advance(c, slice(6, 8), slice(0, 16))
 
         def forward_x(c):
             return inner_coef * (V[c, 3:7] - V[c, 2:6]) - outer_coef * (V[c, 4:8] - V[c, 1:5])
@@ -372,10 +399,10 @@
         ve, vn, vd = (V[c, 2:6] for c in range(3))
         exx = backward_x(0)
         eyy = backward_rows(vn)
-        ezz = backward_lanes(vd)
-        exz = forward_lanes(ve) + forward_x(2)
+        ezz = depth_of[2]
+        exz = depth_of[0] + forward_x(2)
         exy = forward_rows(ve) + forward_x(1)
-        eyz = forward_lanes(vn) + forward_rows(vd)
+        eyz = depth_of[1] + forward_rows(vd)
         lame, shear = PROP[0], PROP[1]
         volume = lame * (exx + eyy + ezz)
         twice = shear + shear
@@ -413,12 +440,15 @@
                 new = mean + new
             S[c] = jnp.where(own, new, 0.0)
 
-        wait_all(copies, False)
+        wait_all(copies, around, False)
 
         @pl.when(t < STEPS - 1)
         def _():
-            forces()
-            start_all(functools.partial(step_copies, t + 1))
+            later = functools.partial(step_copies, t + 1)
+            rim_forces()
+            start_all(later, diagonal)
+            own_forces()
+            start_all(later, sides)
 
         return carry
 
@@ -467,6 +497,7 @@
             scratch_shapes=[
                 pltpu.VMEM((LAYERS, ROWS, 128), jnp.int32),
                 pltpu.VMEM((3, LAYERS, ROWS, 128), f32),
+                pltpu.VMEM((3, 4, ROWS, 128), f32),
                 pltpu.VMEM((2, 3, LAYERS, ROWS, 128), f32),
                 pltpu.VMEM((2, 3, LAYERS, ROWS, 128), f32),
                 pltpu.VMEM((LAYERS, ROWS, 128), f32),

time: 44.2 us -> 43.7 us (0.989)
  no operation moved by 1% of the time
where the time goes in v4:
time: 43.7 us; the launch traced here: 43.5 us
  Pallas kernels  42.9 us (98%)
  between operations  0.64 us (1%)
    pallas_call x1, Pallas kernels, shards(): pl.pallas_call(functools.partial(kernel, counts), out_shape=(pltpu.VMEM((...  42 us

profile of v4, /device:TPU:6, one launch (start us, length us, event | category | flops | bytes accessed | tf_op | source)
XLA Modules:
  0.0 43.5 jit_solution(13184370494958292145)
XLA Ops:
  0.6 42.0 %shard_map.103 = (f32[3,8,16,128]{3,2,1,0:T(8,128)S(1)}, f32[6,4,16,128]{3,2,1,0:T(8,128)S(1)}, f32[6,4,16,128]{3,2,1,0:T(8,128)S(1)}) custom-call(f32[3,12,4,128]{3,2,1,0:T(4,128)} %bitcast.10, f32[6,12,4,128]{3,2,1,0:T(4,128)} %bitcast.8, f32[6,12,4,128]{3,2,1,0:T(4,128)} %bitcast.9, s32[12,4,128]{2,1,0:T(4,128)} %bitcast.11, f32[3,1,4]{2,1,0:T(1,128)} %bitcast.12, ...), custom_call_target="tpu_custom_call" | custom-call | tf_op jit(solution)/shard_map/pallas_call | solution.py:488
  42.7 0.8 %shard_map.104 = (f32[3,12,4,128]{3,2,1,0:T(4,128)}, f32[6,12,4,128]{3,2,1,0:T(4,128)}, f32[6,12,4,128]{3,2,1,0:T(4,128)}) custom-call(f32[3,8,16,128]{3,2,1,0:T(8,128)S(1)} %get-tuple-element.9.V, f32[6,4,16,128]{3,2,1,0:T(8,128)S(1)} %get-tuple-element.10.S, f32[6,4,16,128]{3,2,1,0:T(8,128)S(1)} %get-tuple-element.11.M), custom_call_target="tpu_custom_call" | custom-call | tf_op jit(solution)/shard_map/pallas_call | solution.py:521

commit v5 on v4

--- a/solution.py
+++ b/solution.py
@@ -293,8 +293,9 @@
     n_x = 1 + has_x[1].astype(jnp.int32) + has_x[-1].astype(jnp.int32)
     n_y = 1 + has_y[1].astype(jnp.int32) + has_y[-1].astype(jnp.int32)
     pl.semaphore_wait(barrier, n_x * n_y - 1)
-    start_all(functools.partial(step_copies, 0), around)
+    start_all(functools.partial(step_copies, 0), diagonal)
     start_all(first_copies, sides)
+    start_all(functools.partial(step_copies, 0), sides)
     for load in small:
         load.wait()
 

time: 43.7 us -> 43.7 us (level)
  no operation moved by 1% of the time
where the time goes in v5:
time: 43.7 us; the launch traced here: 43.5 us
  Pallas kernels  42.9 us (98%)
  between operations  0.64 us (1%)
    pallas_call x1, Pallas kernels, shards(): pl.pallas_call(functools.partial(kernel, counts), out_shape=(pltpu.VMEM((...  42 us

profile of v5, /device:TPU:6, one launch (start us, length us, event | category | flops | bytes accessed | tf_op | source)
XLA Modules:
  0.0 43.5 jit_solution(1579968148320555716)
XLA Ops:
  0.6 42.0 %shard_map.103 = (f32[3,8,16,128]{3,2,1,0:T(8,128)S(1)}, f32[6,4,16,128]{3,2,1,0:T(8,128)S(1)}, f32[6,4,16,128]{3,2,1,0:T(8,128)S(1)}) custom-call(f32[3,12,4,128]{3,2,1,0:T(4,128)} %bitcast.10, f32[6,12,4,128]{3,2,1,0:T(4,128)} %bitcast.8, f32[6,12,4,128]{3,2,1,0:T(4,128)} %bitcast.9, s32[12,4,128]{2,1,0:T(4,128)} %bitcast.11, f32[3,1,4]{2,1,0:T(1,128)} %bitcast.12, ...), custom_call_target="tpu_custom_call" | custom-call | tf_op jit(solution)/shard_map/pallas_call | solution.py:489
  42.7 0.8 %shard_map.104 = (f32[3,12,4,128]{3,2,1,0:T(4,128)}, f32[6,12,4,128]{3,2,1,0:T(4,128)}, f32[6,12,4,128]{3,2,1,0:T(4,128)}) custom-call(f32[3,8,16,128]{3,2,1,0:T(8,128)S(1)} %get-tuple-element.9.V, f32[6,4,16,128]{3,2,1,0:T(8,128)S(1)} %get-tuple-element.10.S, f32[6,4,16,128]{3,2,1,0:T(8,128)S(1)} %get-tuple-element.11.M), custom_call_target="tpu_custom_call" | custom-call | tf_op jit(solution)/shard_map/pallas_call | solution.py:522
